TPU v7x, 256 devices: a whole 4x4x8 slice. The times are simulated.
256 devices in a mesh: grp: 32 (over y, z_hi, core), tp: 8 (over x, z_lo).
Axes of the slice: x: 4, y: 4, z: 8 (z_hi: 4, z_lo: 2; z = z_hi * 2 + z_lo), core: 2. Of those that a mesh axis runs over, the one named last changes fastest.
Arguments:
- pool_pages: bfloat16 [32, 48, 128, 576], P('grp', 'tp'), may hold values from -6 to 6
- page_table: int32 [32, 48], replicated, may hold values from 0 to 47, each once within a row
- read_list: int32 [32, 4], replicated, may hold values from 0 to 31, as said below
- context: int32 [384], P('grp'), may hold values from 1 to 6144, as said below
- queries: bfloat16 [384, 4, 64, 576], P('grp', None, 'tp')
- tail_keys: bfloat16 [384, 4, 576], P('grp')
- residual: bfloat16 [384, 4, 3584], P('grp')
- w_uv: bfloat16 [64, 512, 128], P('tp'), may hold values from -0.25 to 0.25
- w_out: bfloat16 [8192, 3584], P('tp'), may hold values from -0.0625 to 0.0625
- norm_gain: float32 [3584], replicated, may hold values from 0.1 to 1.9
- w_gate: bfloat16 [3584, 1024], P(None, 'tp'), may hold values from -0.09375 to 0.09375
- w_up: bfloat16 [3584, 1024], P(None, 'tp'), may hold values from -0.09375 to 0.09375
- w_down: bfloat16 [1024, 3584], P('tp'), may hold values from -0.1875 to 0.1875
Outputs:
- layer_out: bfloat16 [384, 4, 3584], P('grp', None, 'tp')
Inputs may be any that keep to these rules, and one draw needn't show every extreme that they name: `read_list`: row g names 4 different prefixes; each column names every prefix once. `page_table`: each row names every logical page once. `context`: some request has the full length 6144.
All inputs are finite; a program needn't handle non-finite values.
Results may differ from a plain program's by a relative error of at most 0.02.
Values may be sent and summed in bfloat16 or wider, within the bound.
A program may use at most 128 MiB of HBM per device.

v0:
```python
import jax
import jax.numpy as jnp
from jax import lax
from jax.sharding import PartitionSpec as P

LATENT = 512


SCALE = 192.0 ** (-0.5)
NEGATIVE = -1e30
EPSILON = 1e-06


def attend(asked_rows, all_keys, logical, lengths, tail_rows, top_of, tail_share):
    page_len = all_keys.shape[2]
    offsets = jnp.arange(page_len, dtype=jnp.int32)
    position = logical[:, :, None] * page_len + offsets[None, None, :]
    visible = position[:, None] < lengths[:, :, None, None]
    scores = (
        jnp.einsum("krshc,kjtc->krshjt", asked_rows, all_keys, preferred_element_type=jnp.float32)
        * SCALE
    )
    scores = jnp.where(visible[:, :, None, None], scores, NEGATIVE)
    draft_len = tail_rows.shape[2]
    causal = jnp.arange(draft_len)[None, :] <= jnp.arange(draft_len)[:, None]
    tail_scores = (
        jnp.einsum("krshc,krzc->krshz", asked_rows, tail_rows, preferred_element_type=jnp.float32)
        * SCALE
    )
    tail_scores = jnp.where(causal[None, None, :, None, :], tail_scores, NEGATIVE)
    row_top = top_of(jnp.maximum(jnp.max(scores, axis=(4, 5)), jnp.max(tail_scores, axis=4)))
    weights = jnp.exp(scores - row_top[..., None, None]).astype(jnp.bfloat16)
    tail_weights = jnp.exp(tail_scores - row_top[..., None]).astype(jnp.bfloat16)
    denominator = jnp.sum(weights, axis=(4, 5), dtype=jnp.float32) + tail_share * jnp.sum(
        tail_weights, axis=4, dtype=jnp.float32
    )
    numerator = jnp.einsum(
        "krshjt,kjtc->krshc", weights, all_keys, preferred_element_type=jnp.float32
    )
    numerator = numerator + tail_share * jnp.einsum(
        "krshz,krzc->krshc", tail_weights, tail_rows, preferred_element_type=jnp.float32
    )
    return (numerator[..., :LATENT], denominator)


def on_device(
    pool_pages,
    page_table,
    read_list,
    context,
    queries,
    tail_keys,
    residual,
    w_uv,
    w_out,
    norm_gain,
    w_gate,
    w_up,
    w_down,
):
    groups = lax.axis_size("grp")
    me_group = lax.axis_index("grp")
    me_rank = lax.axis_index("tp")
    pg_dev = pool_pages.shape[1]
    page_len = pool_pages.shape[2]
    key_width = pool_pages.shape[3]
    piece_len = page_len // groups
    read_count = read_list.shape[1]
    row_count = context.shape[0]
    rows_slot = row_count // read_count
    draft_len = queries.shape[1]
    holdings = lax.all_to_all(
        pool_pages.reshape(pg_dev, page_len, key_width),
        "grp",
        split_axis=1,
        concat_axis=0,
        tiled=True,
    )
    holdings = holdings.reshape(groups, pg_dev, piece_len, key_width)
    outgoing = jnp.take(holdings, read_list.reshape(-1), axis=0).reshape(
        groups, read_count, pg_dev, piece_len, key_width
    )
    arrived = lax.all_to_all(outgoing, "grp", split_axis=0, concat_axis=3, tiled=True)
    arrived = arrived.reshape(read_count, pg_dev, page_len, key_width)
    own_reads = lax.dynamic_index_in_dim(read_list, me_group, 0, keepdims=False)
    tables = jnp.take(page_table, own_reads, axis=0)
    lengths = context.reshape(read_count, rows_slot)
    tail_rows = tail_keys.reshape(read_count, rows_slot, draft_len, key_width)
    all_keys = lax.all_gather(arrived, "tp", axis=1, tiled=True)
    asked_rows = queries.reshape(read_count, rows_slot, draft_len, queries.shape[2], key_width)

    def keep_local(values):
        return values

    numerator, denominator = attend(
        asked_rows, all_keys, tables, lengths, tail_rows, keep_local, 1.0
    )
    latent_out = (numerator / denominator[..., None]).astype(jnp.bfloat16)
    head_out = jnp.einsum(
        "krshl,hlv->krshv", latent_out, w_uv, preferred_element_type=jnp.float32
    ).astype(jnp.bfloat16)
    flat_heads = head_out.reshape(row_count * draft_len, w_uv.shape[0] * w_uv.shape[2])
    partial_mix = jnp.dot(flat_heads, w_out, preferred_element_type=jnp.float32)
    mixed = lax.psum(partial_mix.astype(jnp.bfloat16), "tp").astype(jnp.float32)
    model_width = residual.shape[2]
    hidden = residual.reshape(row_count * draft_len, model_width).astype(jnp.float32) + mixed
    squares = jnp.mean(hidden * hidden, axis=-1, keepdims=True)
    normed = (hidden * lax.rsqrt(squares + EPSILON) * norm_gain).astype(jnp.bfloat16)
    gate_value = jnp.dot(normed, w_gate, preferred_element_type=jnp.float32)
    upward = jnp.dot(normed, w_up, preferred_element_type=jnp.float32)
    activated = (jax.nn.silu(gate_value) * upward).astype(jnp.bfloat16)
    partial_down = jnp.dot(activated, w_down, preferred_element_type=jnp.float32)
    summed = lax.psum(partial_down.astype(jnp.bfloat16), "tp").astype(jnp.float32)
    combined = hidden + summed
    slab_width = model_width // lax.axis_size("tp")
    own_columns = lax.dynamic_slice_in_dim(combined, me_rank * slab_width, slab_width, 1)
    return own_columns.astype(jnp.bfloat16).reshape(row_count, draft_len, slab_width)


def solution(mesh):
    placed = (
        P("grp", "tp", None, None),
        P(),
        P(),
        P("grp"),
        P("grp", None, "tp", None),
        P("grp", None, None),
        P("grp", None, None),
        P("tp", None, None),
        P("tp", None),
        P(),
        P(None, "tp"),
        P(None, "tp"),
        P("tp", None),
    )
    return jax.shard_map(
        on_device, mesh=mesh, in_specs=placed, out_specs=P("grp", None, "tp"), check_vma=False
    )
```

profile of v0, /device:TPU:1, one launch (start us, length us, event | category | flops | bytes accessed | tf_op | source)
XLA Modules:
  0.0 926.0 jit_solution(12921296424359213844)
XLA Ops:
  6.5 2.9 copy.23
  9.5 12.8 %all-to-all-start = ((bf16[6,128,576]{2,0,1:T(8,128)(2,1)}), bf16[6,128,576]{2,0,1:T(8,128)(2,1)S(1)}, u32[]{:S(2)}, u32[]{:S(2)}) async-start(bf16[6,128,576]{2,0,1:T(8,128)(2,1)} %bitcast.80), calls=%async_computation | async-start | bytes 2621440 | tf_op jit(solution)/shard_map/all_to_all | solution.py:72
  22.3 0.8 copy.26
  23.2 0.7 compare_and_fusion
  24.0 32.0 %all-to-all-done = bf16[6,128,576]{2,0,1:T(8,128)(2,1)S(1)} async-done(((bf16[6,128,576]{2,0,1:T(8,128)(2,1)}), bf16[6,128,576]{2,0,1:T(8,128)(2,1)S(1)}, u32[]{:S(2)}, u32[]{:S(2)}) %all-to-all-start) | async-done | bytes 884768 | tf_op jit(solution)/shard_map/all_to_all | solution.py:72
  56.0 0.4 copy.52
  56.4 7.6 gather_fusion.1
  64.0 4.0 broadcast_select_fusion
  68.0 96.3 %all_to_all.30 = bf16[32,4,6,4,576]{4,3,2,1,0:T(4,128)(2,1)S(1)} all-to-all(bf16[32,4,6,4,576]{4,3,2,1,0:T(4,128)(2,1)S(1)} %broadcast_select_fusion), channel_id=1, replica_groups=mesh['grp'=32,'tp'=8] {'grp'}, dimensions={0} | all-to-all | bytes 7077888 | tf_op jit(solution)/shard_map/all_to_all | solution.py:83
  164.3 3.9 copy.27
  168.2 7.9 copy.28
  176.1 0.2 all-reduce.3.cloned.1.call-start
  176.3 0.2 dynamic-slice_reduce_fusion
  176.6 0.6 gather_fusion
  177.4 0.2 broadcast_compare_fusion
  177.6 1.4 fusion.31
  179.0 538.6 %all-gather.2.cloned.1.call-done = bf16[4,48,128,576]{2,3,1,0:T(8,128)(2,1)} async-done(((bf16[4,6,128,576]{2,3,1,0:T(8,128)(2,1)}), bf16[4,48,128,576]{2,3,1,0:T(8,128)(2,1)}) %all-gather.2.cloned.1.call-update) | async-done | bytes 28311568 | tf_op jit(solution)/shard_map/all_gather | solution.py:89
  717.6 15.5 %fusion.4 = (f32[4,3,4,8]{3,2,1,0:T(4,128)S(1)}, f32[4,48,128,3,4,8]{2,5,4,3,1,0:T(8,128)}) fusion(pred[4,3,48,128]{3,1,2,0:T(4,128)(4,1)S(1)} %broadcast_compare_fusion, bf16[4,3,4,8,576,1]{4,3,2,1,5,0:T(8,128)(2,1)S(1)} %bitcast.83, bf16[4,48,128,576]{2,3,1,0:T(8,128)(2,1)} %all-gather.2.cloned.1.call-done), kind=kOutput, calls=%fused_computation.9 | convolution fusion | flops 2724986368 | bytes 38266368 | tf_op jit(solution)/shard_map/krshc,kjtc->krshjt/dot_general | solution.py:20
  733.2 0.1 convert_reduce_fusion.1
  733.3 0.3 fusion.29
  733.6 6.2 convert_reduce_fusion
  739.8 15.5 %fusion.5 = f32[4,3,4,8,576]{4,3,2,1,0:T(8,128)S(1)} fusion(bf16[4,48,128,576]{2,3,1,0:T(8,128)(2,1)} %all-gather.2.cloned.1.call-done, f32[4,48,128,3,4,8]{2,5,4,3,1,0:T(8,128)} %get-tuple-element.8, f32[4,3,4,8]{3,2,1,0:T(4,128)S(1)} %max.11, pred[4,3,48,128]{3,1,2,0:T(4,128)(4,1)S(1)} %broadcast_compare_fusion), kind=kOutput, calls=%fused_computation.13 | convolution fusion | flops 2727346176 | bytes 38708736 | tf_op jit(solution)/shard_map/krshjt,kjtc->krshc/dot_general | solution.py:37
  755.4 0.2 fusion.13
  755.6 0.4 fusion.8
  756.0 5.2 convolution_convert_fusion.1
  761.4 74.1 %all-reduce.3.cloned.1.call-done = bf16[48,3584]{1,0:T(8,128)(2,1)} async-done(((bf16[48,3584]{1,0:T(8,128)(2,1)}), bf16[48,3584]{1,0:T(8,128)(2,1)}) %all-reduce.3.cloned.1.call-update) | async-done | bytes 344080 | tf_op jit(solution)/shard_map/psum | solution.py:104
  835.5 1.2 multiply_reduce_fusion
  836.7 0.3 fusion.30
  837.0 2.8 convolution_convert_fusion
  839.8 78.1 %all-reduce.5.cloned.1.call-done = bf16[48,3584]{1,0:T(8,128)(2,1)} async-done(((bf16[48,3584]{1,0:T(8,128)(2,1)}), bf16[48,3584]{1,0:T(8,128)(2,1)}) %all-reduce.5.cloned.1.call-update) | async-done | bytes 344080 | tf_op jit(solution)/shard_map/psum | solution.py:113
  917.9 0.9 fusion.17
  918.9 0.6 reshape.163
  (39 shorter events, 0.8 us)
Async XLA Ops:
  6.5 749.0 %copy-start = (bf16[8,512,128]{2,1,0:T(8,128)(2,1)S(1)}, bf16[8,512,128]{2,1,0:T(8,128)(2,1)}, u32[]{:S(2)}) copy-start(bf16[8,512,128]{2,1,0:T(8,128)(2,1)} %param.20) | copy-start | bytes 3145732
  9.5 46.5 %all-to-all-start = ((bf16[6,128,576]{2,0,1:T(8,128)(2,1)}), bf16[6,128,576]{2,0,1:T(8,128)(2,1)S(1)}, u32[]{:S(2)}, u32[]{:S(2)}) async-start(bf16[6,128,576]{2,0,1:T(8,128)(2,1)} %bitcast.80), calls=%async_computation | async-start | bytes 2621440 | tf_op jit(solution)/shard_map/all_to_all | solution.py:72
  22.2 695.4 %all-gather.2.cloned.1.call-start = ((), (), s32[]{:S(2)}) async-start(), calls=%async_computation.2 | async-start | bytes 31850496 | tf_op jit(solution)/shard_map/all_gather | solution.py:89
  164.3 12.1 %copy-start.6 = (s32[32,4]{0,1:T(4,128)S(1)}, s32[32,4]{0,1:T(4,128)}, u32[]{:S(2)}) copy-start(s32[32,4]{0,1:T(4,128)} %param.15) | copy-start | bytes 1540
  164.3 12.3 %copy-start.8 = (s32[12]{0:T(128)S(1)}, s32[12]{0:T(128)}, u32[]{:S(2)}) copy-start(s32[12]{0:T(128)} %param.16) | copy-start | bytes 148
  164.3 12.3 %copy-start.7 = (s32[32,48]{1,0:T(8,128)S(1)}, s32[32,48]{1,0:T(8,128)}, u32[]{:S(2)}) copy-start(s32[32,48]{1,0:T(8,128)} %param.14) | copy-start | bytes 18436
  164.3 13.3 %copy-start.2 = (bf16[12,4,8,576]{3,2,1,0:T(8,128)(2,1)S(1)}, bf16[12,4,8,576]{3,2,1,0:T(8,128)(2,1)}, u32[]{:S(2)}) copy-start(bf16[12,4,8,576]{3,2,1,0:T(8,128)(2,1)} %param.17) | copy-start | bytes 1327108
  164.3 13.3 %copy-start.5 = (bf16[12,4,576]{2,1,0:T(4,128)(2,1)S(1)}, bf16[12,4,576]{2,1,0:T(4,128)(2,1)}, u32[]{:S(2)}) copy-start(bf16[12,4,576]{2,1,0:T(4,128)(2,1)} %param.18) | copy-start | bytes 165892
  176.1 659.4 %all-reduce.3.cloned.1.call-start = ((), (), s32[]{:S(2)}) async-start(), calls=%async_computation.3 | async-start | bytes 688128 | tf_op jit(solution)/shard_map/psum | solution.py:104
  755.3 5.9 copy-start.3
  755.5 81.1 %copy-start.1 = (bf16[3584,128]{1,0:T(8,128)(2,1)S(1)}, bf16[3584,128]{1,0:T(8,128)(2,1)}, u32[]{:S(2)}) copy-start(bf16[3584,128]{1,0:T(8,128)(2,1)} %param.23) | copy-start | bytes 2752516
  755.6 81.1 %copy-start.4 = (f32[3584]{0:T(1024)S(1)}, f32[3584]{0:T(1024)}, u32[]{:S(2)}) copy-start(f32[3584]{0:T(1024)} %param.22) | copy-start | bytes 43012
  761.2 156.7 %all-reduce.5.cloned.1.call-start = ((), (), s32[]{:S(2)}) async-start(), calls=%async_computation.4 | async-start | bytes 688128 | tf_op jit(solution)/shard_map/psum | solution.py:113
Sparse Core Ops, SparseCore 0:
  176.2 541.3 all-gather.1
  761.4 74.0 all-reduce.2
  839.9 77.9 all-reduce.4
where the time goes:
time: 931 us; the launch traced here: 926 us
  waiting for transfers between devices  723 us (78%)
  blocking collectives  96.3 us (10%)
  matrix products  41.5 us (4%)
  local copies, waits for them, and re-layouts  25.3 us (3%)
  other arithmetic  13.6 us (1%)
  between operations  13.3 us (1%)
  starting transfers between devices  13.1 us (1%)
    all_gather x1, waiting for transfers between devices, on_device(): all_keys = lax.all_gather(arrived, 'tp', axis=1, tiled=True)  539 us
    all_to_all x1, blocking collectives, on_device(): lax.all_to_all(outgoing, 'grp', split_axis=0, concat_axis=3, tiled=True)  96.3 us
    psum x1, waiting for transfers between devices, on_device(): lax.psum(partial_down.astype(jnp.bfloat16), 'tp').astype(jnp.float32)  78.1 us
    psum x1, waiting for transfers between devices, on_device(): mixed = lax.psum(partial_mix.astype(jnp.bfloat16), 'tp').astype(jnp.float32)  74.1 us
    all_to_all x1, waiting for transfers between devices, on_device(): lax.all_to_all(pool_pages.reshape(pg_dev, page_len, key_width), 'grp', sp...  32 us
  transfers between devices with their start and end apart: 4, of which 4 were waited for; matrix products, arithmetic and copies ran while one was open for 0% of the time, Pallas kernels for 0%

commit v1 on v0

v1 whole, which is shorter than its diff:
```python
import functools

import jax
import jax.numpy as jnp
import numpy as np
from jax import lax
from jax.experimental import pallas as pl
from jax.experimental.pallas import tpu as pltpu
from jax.sharding import PartitionSpec as P

LATENT = 512
SCALE = 192.0 ** (-0.5)
SCALE2 = SCALE * 1.4426950408889634
NEGATIVE = -1e30
EPSILON = 1e-06
MESH = pl.DeviceIdType.MESH
F32 = jnp.float32
BF16 = jnp.bfloat16

GROUPS = 32
QP = 24
EP = 6
NP = QP + EP
WIDE = 640
SLAB = 448
SLABW = 512
ROWS = 48
NT = (((1,), (1,)), ((), ()))


def drain(ref, sem):
    pltpu.make_async_copy(ref, ref, sem).wait()


def iota(shape, dim):
    return lax.broadcasted_iota(jnp.int32, shape, dim)


def kernel(
    inv_ref,
    retk_ref,
    reads_ref,
    send_ref,
    pos_ref,
    gain_ref,
    pool_ref,
    wuv_hbm,
    wout_hbm,
    wgate_hbm,
    wup_hbm,
    wdown_hbm,
    out_ref,
    h1,
    s2,
    q1,
    q2,
    kbuf,
    acc_own,
    acc_peer,
    top,
    den,
    numer_out,
    numer_in,
    lse_out,
    lse_in,
    latent,
    flatm,
    wuv,
    wout,
    wgate,
    wup,
    wdown,
    mix,
    rs1,
    agout,
    ag,
    rs2,
    fin,
    sback,
    rback,
    wsem,
    ksend,
    krecv,
    hsend,
    hrecv,
    zsend,
    zrecv,
    tsend,
    trecv,
):
    g = lax.axis_index("grp")
    t = lax.axis_index("tp")
    x, z = t // 2, t % 2
    right = lax.rem(x + 1, 4)
    left = lax.rem(x + 3, 4)
    across = lax.rem(x + 2, 4)
    right_t = right * 2 + z
    left_t = left * 2 + z
    peer_t = x * 2 + (1 - z)

    barrier = pltpu.get_barrier_semaphore()

    @pl.loop(1, GROUPS)
    def _(d):
        pl.semaphore_signal(
            barrier, inc=1, device_id={"grp": lax.rem(g + d, GROUPS)}, device_id_type=MESH
        )

    @pl.loop(1, 8)
    def _(d):
        pl.semaphore_signal(
            barrier, inc=1, device_id={"tp": lax.rem(t + d, 8)}, device_id_type=MESH
        )

    own_keys = pltpu.make_async_copy(pool_ref, kbuf.at[x], wsem.at[0])
    own_keys.start()
    weights = [
        pltpu.make_async_copy(wuv_hbm, wuv, wsem.at[1]),
        pltpu.make_async_copy(wout_hbm, wout, wsem.at[2]),
        pltpu.make_async_copy(wgate_hbm, wgate, wsem.at[3]),
        pltpu.make_async_copy(wup_hbm, wup, wsem.at[4]),
        pltpu.make_async_copy(wdown_hbm, wdown, wsem.at[5]),
    ]
    for copy in weights:
        copy.start()

    @pl.when(g < NP)
    def _():
        h1[g] = send_ref[g]

    pl.semaphore_wait(barrier, GROUPS - 1 + 7)

    @pl.loop(1, GROUPS)
    def _(d):
        to = lax.rem(g + d, GROUPS)

        @pl.when(to < NP)
        def _():
            pltpu.make_async_remote_copy(
                src_ref=send_ref.at[to],
                dst_ref=h1.at[g],
                send_sem=hsend.at[0],
                recv_sem=hrecv.at[0],
                device_id={"grp": to},
                device_id_type=MESH,
            ).start()

    to_right = pltpu.make_async_remote_copy(
        src_ref=pool_ref,
        dst_ref=kbuf.at[x],
        send_sem=ksend.at[0],
        recv_sem=krecv.at[0],
        device_id={"tp": right_t},
        device_id_type=MESH,
    )
    to_left = pltpu.make_async_remote_copy(
        src_ref=pool_ref,
        dst_ref=kbuf.at[x],
        send_sem=ksend.at[1],
        recv_sem=krecv.at[1],
        device_id={"tp": left_t},
        device_id_type=MESH,
    )
    to_right.start()
    to_left.start()

    @pl.when(g < NP)
    def _():
        drain(h1.at[pl.ds(0, GROUPS - 1)], hrecv.at[0])
        kp = lax.rem(g, 2)
        upper = iota((16, WIDE), 0) < 8

        def picked(to):
            first = h1[inv_ref[2 * kp, to]]
            second = h1[inv_ref[2 * kp + 1, to]]
            return jnp.where(upper, first, second)

        @pl.loop(1, GROUPS)
        def _(d):
            to = lax.rem(g + d, GROUPS)
            s2[to] = picked(to)
            pltpu.make_async_remote_copy(
                src_ref=s2.at[to],
                dst_ref=q1.at[g],
                send_sem=hsend.at[1],
                recv_sem=hrecv.at[1],
                device_id={"grp": to},
                device_id_type=MESH,
            ).start()

        q1[g] = picked(g)

    to_right.wait_recv()
    on_right = pltpu.make_async_remote_copy(
        src_ref=kbuf.at[left, pl.ds(0, 3)],
        dst_ref=kbuf.at[left, pl.ds(0, 3)],
        send_sem=ksend.at[2],
        recv_sem=krecv.at[2],
        device_id={"tp": right_t},
        device_id_type=MESH,
    )
    on_right.start()
    to_left.wait_recv()
    on_left = pltpu.make_async_remote_copy(
        src_ref=kbuf.at[right, pl.ds(3, 3)],
        dst_ref=kbuf.at[right, pl.ds(3, 3)],
        send_sem=ksend.at[3],
        recv_sem=krecv.at[3],
        device_id={"tp": left_t},
        device_id_type=MESH,
    )
    on_left.start()

    @pl.when(g < NP)
    def _():
        drain(q1.at[pl.ds(0, NP - 1)], hrecv.at[1])

    @pl.when(g >= NP)
    def _():
        drain(q1.at[pl.ds(0, NP)], hrecv.at[1])

    swap = pltpu.make_async_remote_copy(
        src_ref=q1.at[pl.ds(0, QP)],
        dst_ref=q2,
        send_sem=zsend.at[0],
        recv_sem=zrecv.at[0],
        device_id={"tp": peer_t},
        device_id_type=MESH,
    )
    swap.start()

    own_keys.wait()
    on_right.wait_recv()
    on_left.wait_recv()

    nq = QP * 16

    def prefix_part(asked, acc):
        def block(b, carry):
            rows = asked[pl.ds(0, QP)].reshape(nq, WIDE)
            lengths = rows[:, 576:577].astype(F32) * 64.0 + rows[:, 608:609].astype(F32)
            keys = kbuf[b].reshape(768, 576)
            scores = lax.dot_general(rows[:, :576], keys, NT, preferred_element_type=F32)
            position = pos_ref[b * 2 + z]
            scores = jnp.where(position < lengths, scores * SCALE2, NEGATIVE)
            old = top[...]
            new = jnp.maximum(old, jnp.max(scores, axis=1, keepdims=True))
            weight = jnp.exp2(scores - new).astype(BF16)
            keep = jnp.exp2(old - new)
            top[...] = new
            den[...] = den[...] * keep + jnp.sum(weight.astype(F32), axis=1, keepdims=True)
            acc[...] = acc[...] * keep + jnp.dot(
                weight, keys[:, :LATENT], preferred_element_type=F32
            )
            return carry

        lax.fori_loop(0, 4, block, 0)

    rows = q1[pl.ds(0, QP)].reshape(nq, WIDE)
    extra = q1[pl.ds(QP, EP)].reshape(EP * 16, WIDE)
    nt = EP * 16
    scores = lax.dot_general(
        rows[:, :576], extra[:, :576], NT, preferred_element_type=F32
    )
    n, m = iota((nq, nt), 0), iota((nq, nt), 1)
    line = (m // 32) * 8 + m % 8
    seen = (line < 12) & (line // 4 == n // 128) & ((m // 8) % 4 == (n // 8) % 4)
    seen = seen & (line % 4 <= (n // 32) % 4)
    scores = jnp.where(seen, scores * SCALE2, NEGATIVE)
    first = jnp.max(scores, axis=1, keepdims=True)
    weight = jnp.where(seen, jnp.exp2(scores - first), 0.0).astype(BF16)
    top[...] = first
    den[...] = jnp.sum(weight.astype(F32), axis=1, keepdims=True)
    acc_own[...] = jnp.dot(weight, extra[:, :LATENT], preferred_element_type=F32)
    prefix_part(q1, acc_own)
    own_top = top[...]
    own_den = den[...]

    swap.wait_recv()
    top[...] = jnp.full((nq, 1), NEGATIVE, F32)
    den[...] = jnp.zeros((nq, 1), F32)
    acc_peer[...] = jnp.zeros_like(acc_peer)
    prefix_part(q2, acc_peer)
    numer_out[...] = (acc_peer[...] / den[...]).astype(BF16)
    lse = top[...] + jnp.log2(den[...])
    diagonal = iota((nq, nq), 0) == iota((nq, nq), 1)
    lse_out[...] = jnp.broadcast_to(
        jnp.sum(jnp.where(diagonal, lse, 0.0), axis=0, keepdims=True), (8, nq)
    )
    back = [
        pltpu.make_async_remote_copy(
            src_ref=numer_out,
            dst_ref=numer_in,
            send_sem=zsend.at[1],
            recv_sem=zrecv.at[1],
            device_id={"tp": peer_t},
            device_id_type=MESH,
        ),
        pltpu.make_async_remote_copy(
            src_ref=lse_out,
            dst_ref=lse_in,
            send_sem=zsend.at[2],
            recv_sem=zrecv.at[2],
            device_id={"tp": peer_t},
            device_id_type=MESH,
        ),
    ]
    for copy in back:
        copy.start()
    for copy in weights:
        copy.wait()
    for copy in back:
        copy.wait_recv()
    lse = jnp.sum(jnp.where(diagonal, lse_in[0:1, :], 0.0), axis=1, keepdims=True)
    both = jnp.maximum(own_top, lse)
    mine = jnp.exp2(own_top - both)
    theirs = jnp.exp2(lse - both)
    scaled = 1.0 / (own_den * mine + theirs)
    latent[...] = (
        acc_own[...] * (mine * scaled) + numer_in[...].astype(F32) * (theirs * scaled)
    ).astype(BF16)

    head_of = iota((nq, 128), 0) % 8
    for h in range(8):
        value = jnp.dot(latent[...], wuv[h], preferred_element_type=F32)
        flatm[:, h * 128 : (h + 1) * 128] = jnp.where(head_of == h, value, 0.0).astype(BF16)
    o, n = iota((ROWS, nq), 0), iota((ROWS, nq), 1)
    chosen = ((n // 32) == o % 12) & ((n // 8) % 4 == o // 12)
    flat = jnp.dot(
        jnp.where(chosen, 1.0, 0.0).astype(BF16), flatm[...], preferred_element_type=F32
    ).astype(BF16)

    def spread(part, dst, s):
        for d in range(1, 8):
            to = lax.rem(t + d, 8)
            pltpu.make_async_remote_copy(
                src_ref=part(to),
                dst_ref=dst.at[t],
                send_sem=tsend.at[s],
                recv_sem=trecv.at[s],
                device_id={"tp": to},
                device_id_type=MESH,
            ).start()

    def slabs(left_side, weight, dst):
        for j in range(4):
            wide = jnp.dot(
                left_side, weight[:, 896 * j : 896 * (j + 1)], preferred_element_type=F32
            ).astype(BF16)
            dst[2 * j, :, :SLAB] = wide[:, :SLAB]
            dst[2 * j + 1, :, :SLAB] = wide[:, SLAB:]

    mix[0, :, :, SLAB:] = jnp.zeros((8, ROWS, SLABW - SLAB), BF16)
    mix[1, :, :, SLAB:] = jnp.zeros((8, ROWS, SLABW - SLAB), BF16)
    slabs(flat, wout, mix.at[0])
    spread(lambda to: mix.at[0, to], rs1, 0)
    rs1[t] = mix[0, t]
    o, m = iota((ROWS, nt), 0), iota((ROWS, nt), 1)
    line = (m // 32) * 8 + m % 8
    chosen = (line - 12 == o % 12) & ((m // 8) % 4 == o // 12)
    hidden = jnp.dot(
        jnp.where(chosen, 1.0, 0.0).astype(BF16),
        extra[:, :SLABW],
        preferred_element_type=F32,
    )
    drain(rs1.at[pl.ds(0, 7)], trecv.at[0])
    for j in range(8):
        hidden = hidden + rs1[j].astype(F32)
    lane = iota((ROWS, SLABW), 1)
    hidden = jnp.where(lane < SLAB, hidden, 0.0)
    square = jnp.sum(hidden * hidden, axis=1, keepdims=True)
    high = square.astype(BF16).astype(F32)
    low = square - high
    packed = jnp.where(
        lane < SLAB, hidden * gain_ref[...], jnp.where(lane < SLAB + 32, high, low)
    ).astype(BF16)
    agout[...] = packed
    spread(lambda to: agout, ag, 1)
    ag[t] = packed
    drain(ag.at[pl.ds(0, 7)], trecv.at[1])
    total = jnp.zeros((ROWS, 1), F32)
    gate = jnp.zeros((ROWS, 128), F32)
    upward = jnp.zeros((ROWS, 128), F32)
    for j in range(8):
        block = ag[j]
        total = total + (
            block[:, SLAB : SLAB + 1].astype(F32) + block[:, SLAB + 32 : SLAB + 33].astype(F32)
        )
        at = slice(SLAB * j, SLAB * (j + 1))
        gate = gate + jnp.dot(block[:, :SLAB], wgate[at], preferred_element_type=F32)
        upward = upward + jnp.dot(block[:, :SLAB], wup[at], preferred_element_type=F32)
    factor = lax.rsqrt(total * (1.0 / 3584.0) + EPSILON)
    gate = gate * factor
    upward = upward * factor
    active = (gate / (1.0 + jnp.exp(-gate)) * upward).astype(BF16)
    slabs(active, wdown, mix.at[1])
    spread(lambda to: mix.at[1, to], rs2, 2)
    rs2[t] = mix[1, t]
    drain(rs2.at[pl.ds(0, 7)], trecv.at[2])
    for j in range(8):
        hidden = hidden + rs2[j].astype(F32)

    o, m = iota((64, ROWS), 0), iota((64, ROWS), 1)
    chosen = (o // 16 == m // 12) & (o % 16 == m % 12)
    fin[...] = (
        jnp.dot(
            jnp.where(chosen, 1.0, 0.0).astype(BF16),
            hidden.astype(BF16),
            preferred_element_type=F32,
        )
        .astype(BF16)
        .reshape(4, 16, SLABW)
    )

    @pl.loop(1, GROUPS)
    def _(d):
        to = lax.rem(g + d, GROUPS)
        sback[to] = fin[retk_ref[to]]
        pltpu.make_async_remote_copy(
            src_ref=sback.at[to],
            dst_ref=rback.at[g],
            send_sem=hsend.at[2],
            recv_sem=hrecv.at[2],
            device_id={"grp": to},
            device_id_type=MESH,
        ).start()

    rback[g] = fin[retk_ref[g]]
    drain(rback.at[pl.ds(0, GROUPS - 1)], hrecv.at[2])
    for k in range(4):
        out_ref[k] = rback[reads_ref[k]][:, :SLAB]

    @pl.when(g >= NP)
    def _():
        drain(send_ref.at[pl.ds(0, NP)], hsend.at[0])

    @pl.when(g < NP)
    def _():
        drain(send_ref.at[pl.ds(0, NP - 1)], hsend.at[0])
        drain(s2.at[pl.ds(0, GROUPS - 1)], hsend.at[1])

    drain(sback.at[pl.ds(0, GROUPS - 1)], hsend.at[2])
    to_right.wait_send()
    to_left.wait_send()
    on_right.wait_send()
    on_left.wait_send()
    swap.wait_send()
    for copy in back:
        copy.wait_send()
    for s in range(3):
        drain(rs1.at[pl.ds(0, 7)], tsend.at[s])


def on_device(
    pool_pages,
    page_table,
    read_list,
    context,
    queries,
    tail_keys,
    residual,
    w_uv,
    w_out,
    norm_gain,
    w_gate,
    w_up,
    w_down,
):
    g = lax.axis_index("grp")
    t = lax.axis_index("tp")
    asked = queries.reshape(4, 3, 4, 8, 576).transpose(1, 2, 0, 3, 4)
    marks = context.reshape(4, 3).T[:, None, :, None, None]
    marks = jnp.concatenate(
        [
            jnp.broadcast_to(marks // 64, (3, 4, 4, 8, 32)),
            jnp.broadcast_to(marks % 64, (3, 4, 4, 8, 32)),
        ],
        axis=-1,
    ).astype(BF16)
    asked = jnp.concatenate([asked, marks], axis=-1).reshape(QP, 16, WIDE)
    tail = jnp.pad(tail_keys.reshape(4, 12, 576), ((0, 0), (0, 0), (0, WIDE - 576)))
    slab = lax.dynamic_slice_in_dim(residual, t * SLAB, SLAB, 2).reshape(4, 12, SLAB)
    slab = jnp.pad(slab, ((0, 0), (0, 0), (0, WIDE - SLAB)))
    extra = jnp.concatenate([tail, slab], axis=1).reshape(4, 3, 8, WIDE)
    extra = extra.transpose(1, 0, 2, 3).reshape(EP, 16, WIDE)
    send = jnp.concatenate([asked, extra], axis=0)

    every = jnp.arange(GROUPS, dtype=jnp.int32)
    hit = read_list.T[:, :, None] == every[None, None, :]
    inv = jnp.sum(jnp.where(hit, every[None, :, None], 0), axis=1).astype(jnp.int32)
    retk = jnp.sum(
        jnp.where(read_list == g, jnp.arange(4, dtype=jnp.int32)[None, :], 0), axis=1
    ).astype(jnp.int32)
    reads = lax.dynamic_index_in_dim(read_list, g, 0, keepdims=False)
    table = lax.dynamic_index_in_dim(page_table, g, 0, keepdims=False)
    pos = (table[:, None] * 128 + jnp.arange(128, dtype=jnp.int32)[None, :]).astype(F32)
    pos = pos.reshape(8, 1, 768)
    gain = lax.dynamic_slice_in_dim(norm_gain, t * SLAB, SLAB, 0)
    gain = jnp.pad(gain, (0, SLABW - SLAB)).reshape(1, SLABW)

    smem = pl.BlockSpec(memory_space=pltpu.SMEM)
    vmem = pl.BlockSpec(memory_space=pltpu.VMEM)
    anym = pl.BlockSpec(memory_space=pl.ANY)
    dma = pltpu.SemaphoreType.DMA
    nq = QP * 16
    done = pl.pallas_call(
        kernel,
        out_shape=jax.ShapeDtypeStruct((4, 16, SLAB), BF16),
        in_specs=[smem] * 3 + [vmem] * 3 + [anym] * 6,
        out_specs=vmem,
        scratch_shapes=[
            pltpu.VMEM((GROUPS, 16, WIDE), BF16),
            pltpu.VMEM((GROUPS, 16, WIDE), BF16),
            pltpu.VMEM((NP, 16, WIDE), BF16),
            pltpu.VMEM((QP, 16, WIDE), BF16),
            pltpu.VMEM((4, 6, 128, 576), BF16),
            pltpu.VMEM((nq, LATENT), F32),
            pltpu.VMEM((nq, LATENT), F32),
            pltpu.VMEM((nq, 1), F32),
            pltpu.VMEM((nq, 1), F32),
            pltpu.VMEM((nq, LATENT), BF16),
            pltpu.VMEM((nq, LATENT), BF16),
            pltpu.VMEM((8, nq), F32),
            pltpu.VMEM((8, nq), F32),
            pltpu.VMEM((nq, LATENT), BF16),
            pltpu.VMEM((nq, 1024), BF16),
            pltpu.VMEM((8, 512, 128), BF16),
            pltpu.VMEM((1024, 3584), BF16),
            pltpu.VMEM((3584, 128), BF16),
            pltpu.VMEM((3584, 128), BF16),
            pltpu.VMEM((128, 3584), BF16),
            pltpu.VMEM((2, 8, ROWS, SLABW), BF16),
            pltpu.VMEM((8, ROWS, SLABW), BF16),
            pltpu.VMEM((ROWS, SLABW), BF16),
            pltpu.VMEM((8, ROWS, SLABW), BF16),
            pltpu.VMEM((8, ROWS, SLABW), BF16),
            pltpu.VMEM((4, 16, SLABW), BF16),
            pltpu.VMEM((GROUPS, 16, SLABW), BF16),
            pltpu.VMEM((GROUPS, 16, SLABW), BF16),
            dma((6,)),
            dma((4,)),
            dma((4,)),
            dma((3,)),
            dma((3,)),
            dma((3,)),
            dma((3,)),
            dma((3,)),
            dma((3,)),
        ],
        compiler_params=pltpu.CompilerParams(
            collective_id=0, has_side_effects=True, vmem_limit_bytes=56 * 1024 * 1024
        ),
    )(
        inv,
        retk,
        reads,
        send,
        pos,
        gain,
        pool_pages.reshape(6, 128, 576),
        w_uv,
        w_out,
        w_gate,
        w_up,
        w_down,
    )
    return done[:, :12].reshape(12, 4, SLAB)


def solution(mesh):
    placed = (
        P("grp", "tp", None, None),
        P(),
        P(),
        P("grp"),
        P("grp", None, "tp", None),
        P("grp", None, None),
        P("grp", None, None),
        P("tp", None, None),
        P("tp", None),
        P(),
        P(None, "tp"),
        P(None, "tp"),
        P("tp", None),
    )
    return jax.shard_map(
        on_device, mesh=mesh, in_specs=placed, out_specs=P("grp", None, "tp"), check_vma=False
    )
```

time: 931 us -> 126 us (0.14)
  waiting for transfers between devices: 723 us -> 0 us
  Pallas kernels: 0 us -> 111 us
  blocking collectives: 96.3 us -> 0 us
  matrix products: 41.5 us -> 0 us
  local copies, waits for them, and re-layouts: 25.3 us -> 9.94 us
  between operations: 13.3 us -> 0.08 us
  starting transfers between devices: 13.1 us -> 0 us
    all_gather x1 -> x0, waiting for transfers between devices: 539 us -> none  [on_device(): all_keys = lax.all_gather(arrived, 'tp', axis=1, tiled=True)]
    psum x2 -> x0, waiting for transfers between devices: 152 us -> none  [the longest x1 78.1 us: on_device(): lax.psum(partial_down.astype(jnp.bfloat16), 'tp').astype(jnp.float32)]
    pallas_call x0 -> x1, Pallas kernels: none -> 111 us  [on_device(): pl.pallas_call(kernel, out_shape=jax.ShapeDtypeStruct((4, 16, SLAB), BF16...]
    all_to_all x1 -> x0, blocking collectives: 96.3 us -> none  [on_device(): lax.all_to_all(outgoing, 'grp', split_axis=0, concat_axis=3, tiled=True)]
    dot_general x8 -> x0, matrix products: 41.5 us -> none  [the longest x1 15.5 us: attend(): jnp.einsum('krshc,kjtc->krshjt', asked_rows, all_keys, preferred_element_...]
    all_to_all x1 -> x0, waiting for transfers between devices: 32 us -> none  [on_device(): lax.all_to_all(pool_pages.reshape(pg_dev, page_len, key_width), 'grp', sp...]
    all_to_all x1 -> x0, starting transfers between devices: 12.8 us -> none  [on_device(): lax.all_to_all(pool_pages.reshape(pg_dev, page_len, key_width), 'grp', sp...]
  transfers between devices with their start and end apart: 4 -> 0, of which waited for: 4 -> 0; matrix products, arithmetic and copies ran while one was open for 0% -> 0% of each run, Pallas kernels for 0% -> 0%
where the time goes in v1:
time: 126 us
  Pallas kernels  111 us (88%)
  local copies, waits for them, and re-layouts  9.94 us (8%)
  other arithmetic  5.1 us (4%)
    pallas_call x1, Pallas kernels, on_device(): pl.pallas_call(kernel, out_shape=jax.ShapeDtypeStruct((4, 16, SLAB), BF16...  111 us

profile of v1, /device:TPU:1, one launch (start us, length us, event | category | flops | bytes accessed | tf_op | source)
XLA Modules:
  0.0 126.0 jit_solution(10337820031038177990)
XLA Ops:
  0.0 0.0 copy-start
  0.0 1.3 %select_reduce_fusion.1.retk_ref = s32[32]{0:T(128)} fusion(s32[32,4]{0,1:T(4,128)} %param.15, s32[]{:T(128)S(6)} %axis_index.23), kind=kLoop, calls=%fused_computation.26 | loop fusion | flops 352 | bytes 644 | tf_op jit(solution)/shard_map/reduce_sum | solution.py:491
  1.3 0.7 fusion.10
  2.0 1.4 %dynamic-slice_reduce_fusion.reads_ref = s32[4]{0:T(128)} fusion(s32[32,4]{0,1:T(4,128)} %param.15, s32[]{:T(128)S(6)} %select_n.34), kind=kLoop, calls=%fused_computation.25 | loop fusion | bytes 36 | tf_op jit(solution)/shard_map/jit(dynamic_index_in_dim)/dynamic_slice | solution.py:494
  3.4 0.7 reshape.111
  4.2 0.1 copy.33
  4.3 0.1 copy.34
  4.4 0.8 dynamic_slice.17
  5.2 0.6 pad.14
  5.8 1.4 %select_reduce_fusion.inv_ref = s32[4,32]{1,0:T(4,128)} fusion(s32[4,32]{1,0:T(4,128)} %bitcast.46), kind=kLoop, calls=%fused_computation.9 | loop fusion | flops 12160 | bytes 1024 | tf_op jit(solution)/shard_map/reduce_sum | solution.py:490
  7.1 0.1 mul.21
  7.2 0.1 copy.36
  7.3 0.1 broadcast_bitcast_fusion
  7.4 0.6 fusion.4.pos_ref
  8.0 0.0 copy-done
  8.0 0.1 constant_dynamic-slice_fusion.1
  8.1 0.9 reshape.113
  9.1 0.1 broadcast_in_dim.46
  9.2 0.1 broadcast_in_dim.45
  9.3 1.1 copy.44
  10.3 0.1 pad_maximum_fusion.1
  10.5 0.9 pad_maximum_fusion.send_ref
  11.4 2.2 %copy.39 = bf16[1,6,128,576]{3,2,1,0:T(8,128)(2,1)} copy(bf16[1,6,128,576]{2,3,1,0:T(8,128)(2,1)} %param.13) | data formatting | bytes 1769472 | tf_op args[0]
  13.6 110.9 %shard_map.127 = bf16[4,16,448]{2,1,0:T(8,128)(2,1)} custom-call(s32[4,32]{1,0:T(4,128)} %select_reduce_fusion.inv_ref, s32[32]{0:T(128)} %select_reduce_fusion.1.retk_ref, s32[4]{0:T(128)} %dynamic-slice_reduce_fusion.reads_ref, bf16[30,16,640]{2,1,0:T(8,128)(2,1)} %pad_maximum_fusion.send_ref, f32[8,1,768]{2,1,0:T(1,128)} %fusion.4.pos_ref, ...), custom_call_target="tpu_custom_call" | custom-call | tf_op jit(solution)/shard_map/pallas_call | solution.py:506
  124.5 1.5 %reshape.119 = bf16[12,4,448]{2,1,0:T(4,128)(2,1)} reshape(bf16[4,12,448]{2,1,0:T(8,128)(2,1)} %bitcast.45) | data formatting | bytes 86016 | tf_op jit(solution)/shard_map/reshape | solution.py:567
  (5 shorter events, 0.1 us)
Async XLA Ops:
  0.0 8.0 %copy-start = (bf16[12,4,3584]{2,1,0:T(4,128)(2,1)S(1)}, bf16[12,4,3584]{2,1,0:T(4,128)(2,1)}, u32[]{:S(2)}) copy-start(bf16[12,4,3584]{2,1,0:T(4,128)(2,1)} %param.19) | copy-start | bytes 1032196

commit v2 on v1

--- a/solution.py
+++ b/solution.py
@@ -25,6 +25,7 @@
 SLAB = 448
 SLABW = 512
 ROWS = 48
+RET = 384
 NT = (((1,), (1,)), ((), ()))
 
 
@@ -37,11 +38,13 @@
 
 
 def kernel(
-    inv_ref,
-    retk_ref,
     reads_ref,
-    send_ref,
-    pos_ref,
+    table_ref,
+    context_ref,
+    reads_vec,
+    queries_ref,
+    tail_ref,
+    resid_ref,
     gain_ref,
     pool_ref,
     wuv_hbm,
@@ -50,6 +53,11 @@
     wup_hbm,
     wdown_hbm,
     out_ref,
+    send_ref,
+    inv_vec,
+    inv_ref,
+    pos_ref,
+    gain_slab,
     h1,
     s2,
     q1,
@@ -57,8 +65,10 @@
     kbuf,
     acc_own,
     acc_peer,
-    top,
-    den,
+    own_top,
+    own_den,
+    peer_top,
+    peer_den,
     numer_out,
     numer_in,
     lse_out,
@@ -98,6 +108,12 @@
     left_t = left * 2 + z
     peer_t = x * 2 + (1 - z)
 
+    pending = {}
+
+    def finish(*names):
+        for name in names or list(pending):
+            pending.pop(name)()
+
     barrier = pltpu.get_barrier_semaphore()
 
     @pl.loop(1, GROUPS)
@@ -123,6 +139,45 @@
     ]
     for copy in weights:
         copy.start()
+    pending["own_keys"] = own_keys.wait
+    pending["weights"] = lambda: [copy.wait() for copy in weights]
+
+    half = iota((8, 64), 1) < 32
+    for k in range(0, 4, 2):
+        for r in range(3):
+            marks = []
+            for n in (k * 3 + r, (k + 1) * 3 + r):
+                length = context_ref[n]
+                marks.append(
+                    jnp.where(half, length // 64, length % 64).astype(F32).astype(BF16)
+                )
+            for s in range(4):
+                i = (r * 4 + s) * 2 + k // 2
+                send_ref[i, 0:8, 0:576] = queries_ref[k * 3 + r, s]
+                send_ref[i, 8:16, 0:576] = queries_ref[(k + 1) * 3 + r, s]
+                send_ref[i, 0:8, 576:] = marks[0]
+                send_ref[i, 8:16, 576:] = marks[1]
+    for j in range(8):
+
+        @pl.when(t == j)
+        def _():
+            at = slice(SLAB * j, SLAB * (j + 1))
+            gain_slab[:, :SLAB] = gain_ref[:, at]
+            gain_slab[:, SLAB:] = jnp.zeros((1, SLABW - SLAB), F32)
+            for k in range(0, 4, 2):
+
+                def line(n, b):
+                    if b < 3:
+                        block = tail_ref[n * 3 + b].astype(F32)
+                    else:
+                        block = resid_ref[n * 3 + b - 3, :, at].astype(F32)
+                    return jnp.pad(block, ((0, 0), (0, WIDE - block.shape[1])))
+
+                for e in range(3):
+                    send_ref[QP + e * 2 + k // 2] = jnp.concatenate(
+                        [line(k, 2 * e), line(k, 2 * e + 1), line(k + 1, 2 * e), line(k + 1, 2 * e + 1)],
+                        axis=0,
+                    ).astype(BF16)
 
     @pl.when(g < NP)
     def _():
@@ -145,6 +200,39 @@
                 device_id_type=MESH,
             ).start()
 
+    def hop1_sent():
+        @pl.when(g >= NP)
+        def _():
+            drain(send_ref.at[pl.ds(0, NP)], hsend.at[0])
+
+        @pl.when(g < NP)
+        def _():
+            drain(send_ref.at[pl.ds(0, NP - 1)], hsend.at[0])
+
+    def hop1_arrived():
+        @pl.when(g < NP)
+        def _():
+            drain(h1.at[pl.ds(0, GROUPS - 1)], hrecv.at[0])
+
+    pending["hop1_sent"] = hop1_sent
+    pending["hop1"] = hop1_arrived
+
+    place, group = iota((GROUPS, 128), 1), iota((GROUPS, 128), 0)
+    inv_vec[...] = jnp.zeros((8, 128), jnp.int32)
+    for k in range(4):
+        asked_here = reads_vec[:, k : k + 1] == place
+        inv_vec[k : k + 1, :] = jnp.max(
+            jnp.where(asked_here, group, 0), axis=0, keepdims=True
+        )
+    askers = pltpu.make_async_copy(inv_vec, inv_ref, wsem.at[6])
+    askers.start()
+    offset = iota((1, 128), 1)
+    for j in range(48):
+        pos_ref[j // 6, :, (j % 6) * 128 : (j % 6 + 1) * 128] = (
+            table_ref[g, j] * 128 + offset
+        ).astype(F32)
+    askers.wait()
+
     to_right = pltpu.make_async_remote_copy(
         src_ref=pool_ref,
         dst_ref=kbuf.at[x],
@@ -163,10 +251,14 @@
     )
     to_right.start()
     to_left.start()
-
+    pending["right_sent"] = to_right.wait_send
+    pending["left_sent"] = to_left.wait_send
+    pending["from_left"] = to_right.wait_recv
+    pending["from_right"] = to_left.wait_recv
+
+    finish("hop1")
     @pl.when(g < NP)
     def _():
-        drain(h1.at[pl.ds(0, GROUPS - 1)], hrecv.at[0])
         kp = lax.rem(g, 2)
         upper = iota((16, WIDE), 0) < 8
 
@@ -190,7 +282,24 @@
 
         q1[g] = picked(g)
 
-    to_right.wait_recv()
+    def hop2_sent():
+        @pl.when(g < NP)
+        def _():
+            drain(s2.at[pl.ds(0, GROUPS - 1)], hsend.at[1])
+
+    def hop2_arrived():
+        @pl.when(g < NP)
+        def _():
+            drain(q1.at[pl.ds(0, NP - 1)], hrecv.at[1])
+
+        @pl.when(g >= NP)
+        def _():
+            drain(q1.at[pl.ds(0, NP)], hrecv.at[1])
+
+    pending["hop2_sent"] = hop2_sent
+    pending["hop2"] = hop2_arrived
+
+    finish("from_left")
     on_right = pltpu.make_async_remote_copy(
         src_ref=kbuf.at[left, pl.ds(0, 3)],
         dst_ref=kbuf.at[left, pl.ds(0, 3)],
@@ -200,7 +309,7 @@
         device_id_type=MESH,
     )
     on_right.start()
-    to_left.wait_recv()
+    finish("from_right")
     on_left = pltpu.make_async_remote_copy(
         src_ref=kbuf.at[right, pl.ds(3, 3)],
         dst_ref=kbuf.at[right, pl.ds(3, 3)],
@@ -210,34 +319,36 @@
         device_id_type=MESH,
     )
     on_left.start()
-
-    @pl.when(g < NP)
-    def _():
-        drain(q1.at[pl.ds(0, NP - 1)], hrecv.at[1])
-
-    @pl.when(g >= NP)
-    def _():
-        drain(q1.at[pl.ds(0, NP)], hrecv.at[1])
-
-    swap = pltpu.make_async_remote_copy(
-        src_ref=q1.at[pl.ds(0, QP)],
-        dst_ref=q2,
-        send_sem=zsend.at[0],
-        recv_sem=zrecv.at[0],
-        device_id={"tp": peer_t},
-        device_id_type=MESH,
-    )
-    swap.start()
-
-    own_keys.wait()
-    on_right.wait_recv()
-    on_left.wait_recv()
+    pending["on_right_sent"] = on_right.wait_send
+    pending["on_left_sent"] = on_left.wait_send
+    pending["across_1"] = on_right.wait_recv
+    pending["across_2"] = on_left.wait_recv
+    finish("hop2")
+
+    swaps = [
+        pltpu.make_async_remote_copy(
+            src_ref=q1.at[pl.ds(8 * c, 8)],
+            dst_ref=q2.at[pl.ds(8 * c, 8)],
+            send_sem=zsend.at[c],
+            recv_sem=zrecv.at[c],
+            device_id={"tp": peer_t},
+            device_id_type=MESH,
+        )
+        for c in range(3)
+    ]
+    for c in range(3):
+        swaps[c].start()
+        pending["swap_sent", c] = swaps[c].wait_send
+        pending["swap", c] = swaps[c].wait_recv
+
+    finish("own_keys", "across_1", "across_2")
 
     nq = QP * 16
 
-    def prefix_part(asked, acc):
+    def prefix_part(asked, acc, top, den):
         def block(b, carry):
-            rows = asked[pl.ds(0, QP)].reshape(nq, WIDE)
+            rows = asked[...]
+            rows = rows.reshape(rows.shape[0] * 16, WIDE)
             lengths = rows[:, 576:577].astype(F32) * 64.0 + rows[:, 608:609].astype(F32)
             keys = kbuf[b].reshape(768, 576)
             scores = lax.dot_general(rows[:, :576], keys, NT, preferred_element_type=F32)
@@ -269,56 +380,47 @@
     scores = jnp.where(seen, scores * SCALE2, NEGATIVE)
     first = jnp.max(scores, axis=1, keepdims=True)
     weight = jnp.where(seen, jnp.exp2(scores - first), 0.0).astype(BF16)
-    top[...] = first
-    den[...] = jnp.sum(weight.astype(F32), axis=1, keepdims=True)
+    own_top[...] = first
+    own_den[...] = jnp.sum(weight.astype(F32), axis=1, keepdims=True)
     acc_own[...] = jnp.dot(weight, extra[:, :LATENT], preferred_element_type=F32)
-    prefix_part(q1, acc_own)
-    own_top = top[...]
-    own_den = den[...]
-
-    swap.wait_recv()
-    top[...] = jnp.full((nq, 1), NEGATIVE, F32)
-    den[...] = jnp.zeros((nq, 1), F32)
-    acc_peer[...] = jnp.zeros_like(acc_peer)
-    prefix_part(q2, acc_peer)
-    numer_out[...] = (acc_peer[...] / den[...]).astype(BF16)
-    lse = top[...] + jnp.log2(den[...])
-    diagonal = iota((nq, nq), 0) == iota((nq, nq), 1)
-    lse_out[...] = jnp.broadcast_to(
-        jnp.sum(jnp.where(diagonal, lse, 0.0), axis=0, keepdims=True), (8, nq)
-    )
-    back = [
-        pltpu.make_async_remote_copy(
-            src_ref=numer_out,
-            dst_ref=numer_in,
-            send_sem=zsend.at[1],
-            recv_sem=zrecv.at[1],
-            device_id={"tp": peer_t},
-            device_id_type=MESH,
-        ),
-        pltpu.make_async_remote_copy(
-            src_ref=lse_out,
-            dst_ref=lse_in,
-            send_sem=zsend.at[2],
-            recv_sem=zrecv.at[2],
-            device_id={"tp": peer_t},
-            device_id_type=MESH,
-        ),
-    ]
-    for copy in back:
-        copy.start()
-    for copy in weights:
-        copy.wait()
-    for copy in back:
-        copy.wait_recv()
-    lse = jnp.sum(jnp.where(diagonal, lse_in[0:1, :], 0.0), axis=1, keepdims=True)
-    both = jnp.maximum(own_top, lse)
-    mine = jnp.exp2(own_top - both)
-    theirs = jnp.exp2(lse - both)
-    scaled = 1.0 / (own_den * mine + theirs)
-    latent[...] = (
-        acc_own[...] * (mine * scaled) + numer_in[...].astype(F32) * (theirs * scaled)
-    ).astype(BF16)
+    prefix_part(q1.at[pl.ds(0, QP)], acc_own, own_top, own_den)
+
+    diagonal = iota((128, 128), 0) == iota((128, 128), 1)
+    for c in range(3):
+        finish(("swap", c))
+        peer_top[...] = jnp.full((128, 1), NEGATIVE, F32)
+        peer_den[...] = jnp.zeros((128, 1), F32)
+        acc_peer[...] = jnp.zeros_like(acc_peer)
+        prefix_part(q2.at[pl.ds(8 * c, 8)], acc_peer, peer_top, peer_den)
+        numer_out[c] = (acc_peer[...] / peer_den[...]).astype(BF16)
+        lse = peer_top[...] + jnp.log2(peer_den[...])
+        lse_out[c] = jnp.broadcast_to(
+            jnp.sum(jnp.where(diagonal, lse, 0.0), axis=0, keepdims=True), (8, 128)
+        )
+        for s, (src, dst) in enumerate([(numer_out, numer_in), (lse_out, lse_in)]):
+            copy = pltpu.make_async_remote_copy(
+                src_ref=src.at[c],
+                dst_ref=dst.at[c],
+                send_sem=zsend.at[3 + 2 * c + s],
+                recv_sem=zrecv.at[3 + 2 * c + s],
+                device_id={"tp": peer_t},
+                device_id_type=MESH,
+            )
+            copy.start()
+            pending["back_sent", c, s] = copy.wait_send
+            pending["back", c, s] = copy.wait_recv
+    finish("weights")
+    for c in range(3):
+        finish(("back", c, 0), ("back", c, 1))
+        at = slice(128 * c, 128 * (c + 1))
+        lse = jnp.sum(jnp.where(diagonal, lse_in[c, 0:1, :], 0.0), axis=1, keepdims=True)
+        both = jnp.maximum(own_top[at], lse)
+        mine = jnp.exp2(own_top[at] - both)
+        theirs = jnp.exp2(lse - both)
+        scaled = 1.0 / (own_den[at] * mine + theirs)
+        latent[at] = (
+            acc_own[at] * (mine * scaled) + numer_in[c].astype(F32) * (theirs * scaled)
+        ).astype(BF16)
 
     head_of = iota((nq, 128), 0) % 8
     for h in range(8):
@@ -341,6 +443,8 @@
                 device_id={"tp": to},
                 device_id_type=MESH,
             ).start()
+        pending["spread_sent", s] = lambda: drain(rs1.at[pl.ds(0, 7)], tsend.at[s])
+        pending["spread", s] = lambda: drain(dst.at[pl.ds(0, 7)], trecv.at[s])
 
     def slabs(left_side, weight, dst):
         for j in range(4):
@@ -363,7 +467,7 @@
         extra[:, :SLABW],
         preferred_element_type=F32,
     )
-    drain(rs1.at[pl.ds(0, 7)], trecv.at[0])
+    finish(("spread", 0))
     for j in range(8):
         hidden = hidden + rs1[j].astype(F32)
     lane = iota((ROWS, SLABW), 1)
@@ -372,12 +476,12 @@
     high = square.astype(BF16).astype(F32)
     low = square - high
     packed = jnp.where(
-        lane < SLAB, hidden * gain_ref[...], jnp.where(lane < SLAB + 32, high, low)
+        lane < SLAB, hidden * gain_slab[...], jnp.where(lane < SLAB + 32, high, low)
     ).astype(BF16)
     agout[...] = packed
     spread(lambda to: agout, ag, 1)
     ag[t] = packed
-    drain(ag.at[pl.ds(0, 7)], trecv.at[1])
+    finish(("spread", 1))
     total = jnp.zeros((ROWS, 1), F32)
     gate = jnp.zeros((ROWS, 128), F32)
     upward = jnp.zeros((ROWS, 128), F32)
@@ -396,26 +500,38 @@
     slabs(active, wdown, mix.at[1])
     spread(lambda to: mix.at[1, to], rs2, 2)
     rs2[t] = mix[1, t]
-    drain(rs2.at[pl.ds(0, 7)], trecv.at[2])
+    finish(("spread", 2))
     for j in range(8):
         hidden = hidden + rs2[j].astype(F32)
 
     o, m = iota((64, ROWS), 0), iota((64, ROWS), 1)
-    chosen = (o // 16 == m // 12) & (o % 16 == m % 12)
-    fin[...] = (
-        jnp.dot(
-            jnp.where(chosen, 1.0, 0.0).astype(BF16),
-            hidden.astype(BF16),
+    result = hidden.astype(BF16)
+
+    def placed(chosen, columns):
+        return jnp.dot(
+            jnp.where((o // 16 == m // 12) & chosen, 1.0, 0.0).astype(BF16),
+            columns,
             preferred_element_type=F32,
         )
-        .astype(BF16)
-        .reshape(4, 16, SLABW)
-    )
+
+    wide = placed(o % 16 == m % 12, result[:, :RET])
+    rest = [
+        placed(o % 16 - 12 + 4 * r == m % 12, result[:, RET:SLAB]) for r in range(3)
+    ]
+    rest = jnp.concatenate(rest + [jnp.zeros((64, RET - 192), F32)], axis=1)
+    lower = iota((64, RET), 0) % 16 >= 12
+    fin[...] = jnp.where(lower, rest, wide).astype(BF16).reshape(4, 16, RET)
+
+    def answer(to):
+        slot = jnp.where(reads_ref[to, 3] == g, 3, 0)
+        slot = jnp.where(reads_ref[to, 2] == g, 2, slot)
+        slot = jnp.where(reads_ref[to, 1] == g, 1, slot)
+        return fin[slot]
 
     @pl.loop(1, GROUPS)
     def _(d):
         to = lax.rem(g + d, GROUPS)
-        sback[to] = fin[retk_ref[to]]
+        sback[to] = answer(to)
         pltpu.make_async_remote_copy(
             src_ref=sback.at[to],
             dst_ref=rback.at[g],
@@ -425,30 +541,17 @@
             device_id_type=MESH,
         ).start()
 
-    rback[g] = fin[retk_ref[g]]
-    drain(rback.at[pl.ds(0, GROUPS - 1)], hrecv.at[2])
+    rback[g] = answer(g)
+    pending["return_sent"] = lambda: drain(sback.at[pl.ds(0, GROUPS - 1)], hsend.at[2])
+    pending["return"] = lambda: drain(rback.at[pl.ds(0, GROUPS - 1)], hrecv.at[2])
+    finish("return")
     for k in range(4):
-        out_ref[k] = rback[reads_ref[k]][:, :SLAB]
-
-    @pl.when(g >= NP)
-    def _():
-        drain(send_ref.at[pl.ds(0, NP)], hsend.at[0])
-
-    @pl.when(g < NP)
-    def _():
-        drain(send_ref.at[pl.ds(0, NP - 1)], hsend.at[0])
-        drain(s2.at[pl.ds(0, GROUPS - 1)], hsend.at[1])
-
-    drain(sback.at[pl.ds(0, GROUPS - 1)], hsend.at[2])
-    to_right.wait_send()
-    to_left.wait_send()
-    on_right.wait_send()
-    on_left.wait_send()
-    swap.wait_send()
-    for copy in back:
-        copy.wait_send()
-    for s in range(3):
-        drain(rs1.at[pl.ds(0, 7)], tsend.at[s])
+        block = rback[reads_ref[g, k]].astype(F32)
+        for r in range(3):
+            out_ref[3 * k + r, :, :RET] = block[4 * r : 4 * r + 4].astype(BF16)
+            out_ref[3 * k + r, :, RET:] = block[12:, 64 * r : 64 * r + 64].astype(BF16)
+
+    finish()
 
 
 def on_device(
@@ -466,62 +569,37 @@
     w_up,
     w_down,
 ):
-    g = lax.axis_index("grp")
-    t = lax.axis_index("tp")
-    asked = queries.reshape(4, 3, 4, 8, 576).transpose(1, 2, 0, 3, 4)
-    marks = context.reshape(4, 3).T[:, None, :, None, None]
-    marks = jnp.concatenate(
-        [
-            jnp.broadcast_to(marks // 64, (3, 4, 4, 8, 32)),
-            jnp.broadcast_to(marks % 64, (3, 4, 4, 8, 32)),
-        ],
-        axis=-1,
-    ).astype(BF16)
-    asked = jnp.concatenate([asked, marks], axis=-1).reshape(QP, 16, WIDE)
-    tail = jnp.pad(tail_keys.reshape(4, 12, 576), ((0, 0), (0, 0), (0, WIDE - 576)))
-    slab = lax.dynamic_slice_in_dim(residual, t * SLAB, SLAB, 2).reshape(4, 12, SLAB)
-    slab = jnp.pad(slab, ((0, 0), (0, 0), (0, WIDE - SLAB)))
-    extra = jnp.concatenate([tail, slab], axis=1).reshape(4, 3, 8, WIDE)
-    extra = extra.transpose(1, 0, 2, 3).reshape(EP, 16, WIDE)
-    send = jnp.concatenate([asked, extra], axis=0)
-
-    every = jnp.arange(GROUPS, dtype=jnp.int32)
-    hit = read_list.T[:, :, None] == every[None, None, :]
-    inv = jnp.sum(jnp.where(hit, every[None, :, None], 0), axis=1).astype(jnp.int32)
-    retk = jnp.sum(
-        jnp.where(read_list == g, jnp.arange(4, dtype=jnp.int32)[None, :], 0), axis=1
-    ).astype(jnp.int32)
-    reads = lax.dynamic_index_in_dim(read_list, g, 0, keepdims=False)
-    table = lax.dynamic_index_in_dim(page_table, g, 0, keepdims=False)
-    pos = (table[:, None] * 128 + jnp.arange(128, dtype=jnp.int32)[None, :]).astype(F32)
-    pos = pos.reshape(8, 1, 768)
-    gain = lax.dynamic_slice_in_dim(norm_gain, t * SLAB, SLAB, 0)
-    gain = jnp.pad(gain, (0, SLABW - SLAB)).reshape(1, SLABW)
-
     smem = pl.BlockSpec(memory_space=pltpu.SMEM)
     vmem = pl.BlockSpec(memory_space=pltpu.VMEM)
     anym = pl.BlockSpec(memory_space=pl.ANY)
     dma = pltpu.SemaphoreType.DMA
     nq = QP * 16
-    done = pl.pallas_call(
+    return pl.pallas_call(
         kernel,
-        out_shape=jax.ShapeDtypeStruct((4, 16, SLAB), BF16),
-        in_specs=[smem] * 3 + [vmem] * 3 + [anym] * 6,
+        out_shape=jax.ShapeDtypeStruct((12, 4, SLAB), BF16),
+        in_specs=[smem] * 3 + [vmem] * 5 + [anym] * 6,
         out_specs=vmem,
         scratch_shapes=[
+            pltpu.VMEM((NP, 16, WIDE), BF16),
+            pltpu.VMEM((8, 128), jnp.int32),
+            pltpu.SMEM((8, 128), jnp.int32),
+            pltpu.VMEM((8, 1, 768), F32),
+            pltpu.VMEM((1, SLABW), F32),
             pltpu.VMEM((GROUPS, 16, WIDE), BF16),
             pltpu.VMEM((GROUPS, 16, WIDE), BF16),
             pltpu.VMEM((NP, 16, WIDE), BF16),
             pltpu.VMEM((QP, 16, WIDE), BF16),
             pltpu.VMEM((4, 6, 128, 576), BF16),
             pltpu.VMEM((nq, LATENT), F32),
-            pltpu.VMEM((nq, LATENT), F32),
+            pltpu.VMEM((128, LATENT), F32),
             pltpu.VMEM((nq, 1), F32),
             pltpu.VMEM((nq, 1), F32),
-            pltpu.VMEM((nq, LATENT), BF16),
-            pltpu.VMEM((nq, LATENT), BF16),
-            pltpu.VMEM((8, nq), F32),
-            pltpu.VMEM((8, nq), F32),
+            pltpu.VMEM((128, 1), F32),
+            pltpu.VMEM((128, 1), F32),
+            pltpu.VMEM((3, 128, LATENT), BF16),
+            pltpu.VMEM((3, 128, LATENT), BF16),
+            pltpu.VMEM((3, 8, 128), F32),
+            pltpu.VMEM((3, 8, 128), F32),
             pltpu.VMEM((nq, LATENT), BF16),
             pltpu.VMEM((nq, 1024), BF16),
             pltpu.VMEM((8, 512, 128), BF16),
@@ -534,16 +612,16 @@
             pltpu.VMEM((ROWS, SLABW), BF16),
             pltpu.VMEM((8, ROWS, SLABW), BF16),
             pltpu.VMEM((8, ROWS, SLABW), BF16),
-            pltpu.VMEM((4, 16, SLABW), BF16),
-            pltpu.VMEM((GROUPS, 16, SLABW), BF16),
-            pltpu.VMEM((GROUPS, 16, SLABW), BF16),
-            dma((6,)),
+            pltpu.VMEM((4, 16, RET), BF16),
+            pltpu.VMEM((GROUPS, 16, RET), BF16),
+            pltpu.VMEM((GROUPS, 16, RET), BF16),
+            dma((7,)),
             dma((4,)),
             dma((4,)),
             dma((3,)),
             dma((3,)),
-            dma((3,)),
-            dma((3,)),
+            dma((9,)),
+            dma((9,)),
             dma((3,)),
             dma((3,)),
         ],
@@ -551,12 +629,14 @@
             collective_id=0, has_side_effects=True, vmem_limit_bytes=56 * 1024 * 1024
         ),
     )(
-        inv,
-        retk,
-        reads,
-        send,
-        pos,
-        gain,
+        read_list,
+        page_table,
+        context,
+        read_list,
+        queries,
+        tail_keys,
+        residual,
+        norm_gain.reshape(1, 3584),
         pool_pages.reshape(6, 128, 576),
         w_uv,
         w_out,
@@ -564,7 +644,6 @@
         w_up,
         w_down,
     )
-    return done[:, :12].reshape(12, 4, SLAB)
 
 
 def solution(mesh):

time: 126 us -> 112 us (0.89)
  other arithmetic: 5.1 us -> 0 us
  Pallas kernels: 111 us -> 106 us
  local copies, waits for them, and re-layouts: 9.94 us -> 6.36 us
    pallas_call x1, Pallas kernels: 111 us -> 106 us  [on_device(): pl.pallas_call(kernel, out_shape=jax.ShapeDtypeStruct((12, 4, SLAB), BF16...]
    reshape x5 -> x1, local copies, waits for them, and re-layouts: 4.19 us -> 1.32 us  [on_device(): norm_gain.reshape(1, 3584)]
    unnamed x3, local copies, waits for them, and re-layouts: 2.23 us -> 5.03 us
    reduce_sum x2 -> x0, other arithmetic: 2.65 us -> none  [the longest x1 1.37 us: on_device(): jnp.sum(jnp.where(hit, every[None, :, None], 0), axis=1).astype(jnp.int32)]
    dynamic_slice x3 -> x0, local copies, waits for them, and re-layouts: 2.31 us -> none  [the longest x1 1.44 us: on_device(): reads = lax.dynamic_index_in_dim(read_list, g, 0, keepdims=False)]
where the time goes in v2:
time: 112 us
  Pallas kernels  106 us (95%)
  local copies, waits for them, and re-layouts  6.36 us (6%)
    pallas_call x1, Pallas kernels, on_device(): pl.pallas_call(kernel, out_shape=jax.ShapeDtypeStruct((12, 4, SLAB), BF16...  106 us
    unnamed x3, local copies, waits for them, and re-layouts  5.03 us

profile of v2, /device:TPU:1, one launch (start us, length us, event | category | flops | bytes accessed | tf_op | source)
XLA Modules:
  0.0 112.0 jit_solution(15032788932118227466)
XLA Ops:
  0.0 1.3 %reshape.6.gain_ref = f32[1,3584]{1,0:T(1,128)} reshape(f32[3584]{0:T(1024)} %param.22) | data formatting | bytes 28672 | tf_op jit(solution)/shard_map/reshape | solution.py:639
  1.3 1.4 %copy.15.reads_ref.reads_vec = s32[32,4]{1,0:T(8,128)} copy(s32[32,4]{0,1:T(4,128)} %param.15) | data formatting | bytes 1024 | tf_op args[2]
  2.7 2.2 %copy.14 = bf16[1,6,128,576]{3,2,1,0:T(8,128)(2,1)} copy(bf16[1,6,128,576]{2,3,1,0:T(8,128)(2,1)} %param.13) | data formatting | bytes 1769472 | tf_op args[0]
  4.9 105.6 %shard_map.127 = bf16[12,4,448]{2,1,0:T(4,128)(2,1)} custom-call(s32[32,4]{1,0:T(8,128)} %copy.15.reads_ref.reads_vec, s32[32,48]{1,0:T(8,128)} %table_ref.1, s32[12]{0:T(128)} %context_ref.1, s32[32,4]{1,0:T(8,128)} %copy.15.reads_ref.reads_vec, bf16[12,4,8,576]{3,2,1,0:T(8,128)(2,1)} %queries_ref.1, bf16[12,4,576]{2,1,0:T(4,128)(2,1)} %tail_ref.1, ...), custom_call_target="tpu_custom_call" | custom-call | tf_op jit(solution)/shard_map/pallas_call | solution.py:577
  110.6 1.4 %copy.18 = bf16[12,4,448]{2,1,0:T(4,128)(2,1)} copy(bf16[12,4,448]{2,1,0:T(4,128)(2,1)} %shard_map.127) | data formatting | bytes 86016

commit v3 on v2

--- a/solution.py
+++ b/solution.py
@@ -64,11 +64,7 @@
     q2,
     kbuf,
     acc_own,
-    acc_peer,
-    own_top,
-    own_den,
-    peer_top,
-    peer_den,
+    sbuf,
     numer_out,
     numer_in,
     lse_out,
@@ -93,6 +89,7 @@
     krecv,
     hsend,
     hrecv,
+    qrecv,
     zsend,
     zrecv,
     tsend,
@@ -126,6 +123,17 @@
     def _(d):
         pl.semaphore_signal(
             barrier, inc=1, device_id={"tp": lax.rem(t + d, 8)}, device_id_type=MESH
+        )
+
+    plane = lax.rem(g // 2, 4)
+    turn = 2 * z - 1
+
+    @pl.loop(0, 16)
+    def _(d):
+        far = lax.rem(plane + 2 - (d % 2) * turn, 4)
+        to = (d // 4) * 8 + far * 2 + (d // 2) % 2
+        pl.semaphore_signal(
+            barrier, inc=1, device_id={"grp": to, "tp": peer_t}, device_id_type=MESH
         )
 
     own_keys = pltpu.make_async_copy(pool_ref, kbuf.at[x], wsem.at[0])
@@ -162,7 +170,7 @@
         @pl.when(t == j)
         def _():
             at = slice(SLAB * j, SLAB * (j + 1))
-            gain_slab[:, :SLAB] = gain_ref[:, at]
+            gain_slab[0, :SLAB] = gain_ref[at]
             gain_slab[:, SLAB:] = jnp.zeros((1, SLABW - SLAB), F32)
             for k in range(0, 4, 2):
 
@@ -183,7 +191,7 @@
     def _():
         h1[g] = send_ref[g]
 
-    pl.semaphore_wait(barrier, GROUPS - 1 + 7)
+    pl.semaphore_wait(barrier, GROUPS - 1 + 7 + 16)
 
     @pl.loop(1, GROUPS)
     def _(d):
@@ -219,8 +227,9 @@
 
     place, group = iota((GROUPS, 128), 1), iota((GROUPS, 128), 0)
     inv_vec[...] = jnp.zeros((8, 128), jnp.int32)
+    columns = reads_vec[...].T
     for k in range(4):
-        asked_here = reads_vec[:, k : k + 1] == place
+        asked_here = columns[:, k : k + 1] == place
         inv_vec[k : k + 1, :] = jnp.max(
             jnp.where(asked_here, group, 0), axis=0, keepdims=True
         )
@@ -271,14 +280,30 @@
         def _(d):
             to = lax.rem(g + d, GROUPS)
             s2[to] = picked(to)
-            pltpu.make_async_remote_copy(
-                src_ref=s2.at[to],
-                dst_ref=q1.at[g],
-                send_sem=hsend.at[1],
-                recv_sem=hrecv.at[1],
-                device_id={"grp": to},
-                device_id_type=MESH,
-            ).start()
+            away = lax.rem(lax.rem(to // 2, 4) - plane + 4, 4)
+            crossing = (g < QP) & ((away == 2) | (away == 2 - turn))
+
+            @pl.when(crossing)
+            def _():
+                pltpu.make_async_remote_copy(
+                    src_ref=s2.at[to],
+                    dst_ref=q2.at[g],
+                    send_sem=hsend.at[1],
+                    recv_sem=qrecv.at[g // 8],
+                    device_id={"grp": to, "tp": peer_t},
+                    device_id_type=MESH,
+                ).start()
+
+            @pl.when(jnp.logical_not(crossing))
+            def _():
+                pltpu.make_async_remote_copy(
+                    src_ref=s2.at[to],
+                    dst_ref=q1.at[g],
+                    send_sem=hsend.at[1],
+                    recv_sem=qrecv.at[g // 8],
+                    device_id={"grp": to},
+                    device_id_type=MESH,
+                ).start()
 
         q1[g] = picked(g)
 
@@ -287,17 +312,22 @@
         def _():
             drain(s2.at[pl.ds(0, GROUPS - 1)], hsend.at[1])
 
-    def hop2_arrived():
-        @pl.when(g < NP)
-        def _():
-            drain(q1.at[pl.ds(0, NP - 1)], hrecv.at[1])
-
-        @pl.when(g >= NP)
-        def _():
-            drain(q1.at[pl.ds(0, NP)], hrecv.at[1])
+    def hop2_arrived(c):
+        count = 8 if c < 3 else EP
+
+        @pl.when(g // 8 == c)
+        def _():
+            @pl.when(g < NP)
+            def _():
+                drain(q1.at[pl.ds(0, count - 1)], qrecv.at[c])
+
+        @pl.when((g // 8 != c) | (g >= NP))
+        def _():
+            drain(q1.at[pl.ds(0, count)], qrecv.at[c])
 
     pending["hop2_sent"] = hop2_sent
-    pending["hop2"] = hop2_arrived
+    for c in range(4):
+        pending["hop2", c] = functools.partial(hop2_arrived, c)
 
     finish("from_left")
     on_right = pltpu.make_async_remote_copy(
@@ -323,77 +353,72 @@
     pending["on_left_sent"] = on_left.wait_send
     pending["across_1"] = on_right.wait_recv
     pending["across_2"] = on_left.wait_recv
-    finish("hop2")
-
-    swaps = [
-        pltpu.make_async_remote_copy(
-            src_ref=q1.at[pl.ds(8 * c, 8)],
-            dst_ref=q2.at[pl.ds(8 * c, 8)],
-            send_sem=zsend.at[c],
-            recv_sem=zrecv.at[c],
-            device_id={"tp": peer_t},
-            device_id_type=MESH,
-        )
-        for c in range(3)
-    ]
+    def swap_arrived(c):
+        drain(q2.at[pl.ds(0, 8)], zrecv.at[c])
+
+    def swap_sent(c):
+        drain(q2.at[pl.ds(0, 8)], zsend.at[c])
+
+    near = lax.rem(plane + turn + 4, 4)
+    far = lax.rem(plane + 2, 4)
     for c in range(3):
-        swaps[c].start()
-        pending["swap_sent", c] = swaps[c].wait_send
-        pending["swap", c] = swaps[c].wait_recv
-
+        finish(("hop2", c))
+        for src, dst, at in ((q1, q2, plane), (q1, q2, near), (q2, q1, near), (q2, q1, far)):
+            part = pl.ds(8 * c + 2 * at, 2)
+            pltpu.make_async_remote_copy(
+                src_ref=src.at[part],
+                dst_ref=dst.at[part],
+                send_sem=zsend.at[c],
+                recv_sem=zrecv.at[c],
+                device_id={"tp": peer_t},
+                device_id_type=MESH,
+            ).start()
+        pending["swap_sent", c] = functools.partial(swap_sent, c)
+        pending["swap", c] = functools.partial(swap_arrived, c)
+    finish(("hop2", 3))
     finish("own_keys", "across_1", "across_2")
 
     nq = QP * 16
-
-    def prefix_part(asked, acc, top, den):
-        def block(b, carry):
-            rows = asked[...]
-            rows = rows.reshape(rows.shape[0] * 16, WIDE)
-            lengths = rows[:, 576:577].astype(F32) * 64.0 + rows[:, 608:609].astype(F32)
-            keys = kbuf[b].reshape(768, 576)
-            scores = lax.dot_general(rows[:, :576], keys, NT, preferred_element_type=F32)
-            position = pos_ref[b * 2 + z]
-            scores = jnp.where(position < lengths, scores * SCALE2, NEGATIVE)
-            old = top[...]
-            new = jnp.maximum(old, jnp.max(scores, axis=1, keepdims=True))
-            weight = jnp.exp2(scores - new).astype(BF16)
-            keep = jnp.exp2(old - new)
-            top[...] = new
-            den[...] = den[...] * keep + jnp.sum(weight.astype(F32), axis=1, keepdims=True)
-            acc[...] = acc[...] * keep + jnp.dot(
-                weight, keys[:, :LATENT], preferred_element_type=F32
+    nt = EP * 16
+    extra = q1[pl.ds(QP, EP)].reshape(nt, WIDE)
+
+    def keys_of(b, width):
+        return jnp.concatenate([kbuf[b, j, :width] for j in range(6)], axis=1)
+
+    def attend(rows, buf, tail=None):
+        lengths = rows[:, 576:577].astype(F32) * 64.0 + rows[:, 608:609].astype(F32)
+        top = jnp.full((128, 1), NEGATIVE, F32)
+        if tail is not None:
+            top = jnp.max(tail, axis=1, keepdims=True)
+        for b in range(4):
+            scores = jnp.dot(rows[:, :576], keys_of(b, 576), preferred_element_type=F32)
+            scores = jnp.where(pos_ref[b * 2 + z] < lengths, scores * SCALE2, NEGATIVE)
+            buf[b] = scores
+            top = jnp.maximum(top, jnp.max(scores, axis=1, keepdims=True))
+        den = jnp.zeros((128, 1), F32)
+        acc = jnp.zeros((128, LATENT), F32)
+        if tail is not None:
+            weight = jnp.exp2(tail - top).astype(BF16)
+            den = jnp.sum(weight.astype(F32), axis=1, keepdims=True)
+            acc = jnp.dot(weight, extra[:, :LATENT], preferred_element_type=F32)
+        for b in range(4):
+            weight = jnp.exp2(buf[b] - top).astype(BF16)
+            den = den + jnp.sum(weight.astype(F32), axis=1, keepdims=True)
+            acc = acc + lax.dot_general(
+                weight, keys_of(b, LATENT), NT, preferred_element_type=F32
             )
-            return carry
-
-        lax.fori_loop(0, 4, block, 0)
-
-    rows = q1[pl.ds(0, QP)].reshape(nq, WIDE)
-    extra = q1[pl.ds(QP, EP)].reshape(EP * 16, WIDE)
-    nt = EP * 16
-    scores = lax.dot_general(
-        rows[:, :576], extra[:, :576], NT, preferred_element_type=F32
-    )
-    n, m = iota((nq, nt), 0), iota((nq, nt), 1)
+        return top, den, acc
+
+    diagonal = iota((128, 128), 0) == iota((128, 128), 1)
+    n, m = iota((128, nt), 0), iota((128, nt), 1)
     line = (m // 32) * 8 + m % 8
-    seen = (line < 12) & (line // 4 == n // 128) & ((m // 8) % 4 == (n // 8) % 4)
-    seen = seen & (line % 4 <= (n // 32) % 4)
-    scores = jnp.where(seen, scores * SCALE2, NEGATIVE)
-    first = jnp.max(scores, axis=1, keepdims=True)
-    weight = jnp.where(seen, jnp.exp2(scores - first), 0.0).astype(BF16)
-    own_top[...] = first
-    own_den[...] = jnp.sum(weight.astype(F32), axis=1, keepdims=True)
-    acc_own[...] = jnp.dot(weight, extra[:, :LATENT], preferred_element_type=F32)
-    prefix_part(q1.at[pl.ds(0, QP)], acc_own, own_top, own_den)
-
-    diagonal = iota((128, 128), 0) == iota((128, 128), 1)
+    in_place = (line % 4 <= n // 32) & ((m // 8) % 4 == (n // 8) % 4)
+    own_top, own_den = [], []
     for c in range(3):
         finish(("swap", c))
-        peer_top[...] = jnp.full((128, 1), NEGATIVE, F32)
-        peer_den[...] = jnp.zeros((128, 1), F32)
-        acc_peer[...] = jnp.zeros_like(acc_peer)
-        prefix_part(q2.at[pl.ds(8 * c, 8)], acc_peer, peer_top, peer_den)
-        numer_out[c] = (acc_peer[...] / peer_den[...]).astype(BF16)
-        lse = peer_top[...] + jnp.log2(peer_den[...])
+        top, den, acc = attend(q2[pl.ds(8 * c, 8)].reshape(128, WIDE), sbuf.at[0])
+        numer_out[c] = (acc / den).astype(BF16)
+        lse = top + jnp.log2(den)
         lse_out[c] = jnp.broadcast_to(
             jnp.sum(jnp.where(diagonal, lse, 0.0), axis=0, keepdims=True), (8, 128)
         )
@@ -409,15 +434,24 @@
             copy.start()
             pending["back_sent", c, s] = copy.wait_send
             pending["back", c, s] = copy.wait_recv
+        rows = q1[pl.ds(8 * c, 8)].reshape(128, WIDE)
+        tail = lax.dot_general(
+            rows[:, :576], extra[:, :576], NT, preferred_element_type=F32
+        )
+        tail = jnp.where(in_place & (line // 4 == c), tail * SCALE2, NEGATIVE)
+        top, den, acc = attend(rows, sbuf.at[1], tail)
+        own_top.append(top)
+        own_den.append(den)
+        acc_own[128 * c : 128 * (c + 1)] = acc
     finish("weights")
     for c in range(3):
         finish(("back", c, 0), ("back", c, 1))
         at = slice(128 * c, 128 * (c + 1))
         lse = jnp.sum(jnp.where(diagonal, lse_in[c, 0:1, :], 0.0), axis=1, keepdims=True)
-        both = jnp.maximum(own_top[at], lse)
-        mine = jnp.exp2(own_top[at] - both)
+        both = jnp.maximum(own_top[c], lse)
+        mine = jnp.exp2(own_top[c] - both)
         theirs = jnp.exp2(lse - both)
-        scaled = 1.0 / (own_den[at] * mine + theirs)
+        scaled = 1.0 / (own_den[c] * mine + theirs)
         latent[at] = (
             acc_own[at] * (mine * scaled) + numer_in[c].astype(F32) * (theirs * scaled)
         ).astype(BF16)
@@ -523,9 +557,9 @@
     fin[...] = jnp.where(lower, rest, wide).astype(BF16).reshape(4, 16, RET)
 
     def answer(to):
-        slot = jnp.where(reads_ref[to, 3] == g, 3, 0)
-        slot = jnp.where(reads_ref[to, 2] == g, 2, slot)
-        slot = jnp.where(reads_ref[to, 1] == g, 1, slot)
+        slot = jnp.where(reads_ref[3, to] == g, 3, 0)
+        slot = jnp.where(reads_ref[2, to] == g, 2, slot)
+        slot = jnp.where(reads_ref[1, to] == g, 1, slot)
         return fin[slot]
 
     @pl.loop(1, GROUPS)
@@ -546,7 +580,7 @@
     pending["return"] = lambda: drain(rback.at[pl.ds(0, GROUPS - 1)], hrecv.at[2])
     finish("return")
     for k in range(4):
-        block = rback[reads_ref[g, k]].astype(F32)
+        block = rback[reads_ref[k, g]].astype(F32)
         for r in range(3):
             out_ref[3 * k + r, :, :RET] = block[4 * r : 4 * r + 4].astype(BF16)
             out_ref[3 * k + r, :, RET:] = block[12:, 64 * r : 64 * r + 64].astype(BF16)
@@ -589,13 +623,9 @@
             pltpu.VMEM((GROUPS, 16, WIDE), BF16),
             pltpu.VMEM((NP, 16, WIDE), BF16),
             pltpu.VMEM((QP, 16, WIDE), BF16),
-            pltpu.VMEM((4, 6, 128, 576), BF16),
+            pltpu.VMEM((4, 6, 576, 128), BF16),
             pltpu.VMEM((nq, LATENT), F32),
-            pltpu.VMEM((128, LATENT), F32),
-            pltpu.VMEM((nq, 1), F32),
-            pltpu.VMEM((nq, 1), F32),
-            pltpu.VMEM((128, 1), F32),
-            pltpu.VMEM((128, 1), F32),
+            pltpu.VMEM((2, 4, 128, 768), F32),
             pltpu.VMEM((3, 128, LATENT), BF16),
             pltpu.VMEM((3, 128, LATENT), BF16),
             pltpu.VMEM((3, 8, 128), F32),
@@ -620,6 +650,7 @@
             dma((4,)),
             dma((3,)),
             dma((3,)),
+            dma((4,)),
             dma((9,)),
             dma((9,)),
             dma((3,)),
@@ -629,15 +660,15 @@
             collective_id=0, has_side_effects=True, vmem_limit_bytes=56 * 1024 * 1024
         ),
     )(
-        read_list,
+        read_list.T,
         page_table,
         context,
-        read_list,
+        read_list.T,
         queries,
         tail_keys,
         residual,
-        norm_gain.reshape(1, 3584),
-        pool_pages.reshape(6, 128, 576),
+        norm_gain,
+        pool_pages.reshape(6, 128, 576).transpose(0, 2, 1),
         w_uv,
         w_out,
         w_gate,

time: 112 us -> 103 us (0.920)
  Pallas kernels: 106 us -> 101 us
  local copies, waits for them, and re-layouts: 6.36 us -> 1.44 us
    pallas_call x1, Pallas kernels: 106 us -> 101 us  [on_device(): pl.pallas_call(kernel, out_shape=jax.ShapeDtypeStruct((12, 4, SLAB), BF16...]
    unnamed x3 -> x1, local copies, waits for them, and re-layouts: 5.03 us -> 1.44 us
    reshape x1 -> x0, local copies, waits for them, and re-layouts: 1.32 us -> none  [on_device(): norm_gain.reshape(1, 3584)]
where the time goes in v3:
time: 103 us
  Pallas kernels  101 us (98%)
  local copies, waits for them, and re-layouts  1.44 us (1%)
    pallas_call x1, Pallas kernels, on_device(): pl.pallas_call(kernel, out_shape=jax.ShapeDtypeStruct((12, 4, SLAB), BF16...  101 us

profile of v3, /device:TPU:1, one launch (start us, length us, event | category | flops | bytes accessed | tf_op | source)
XLA Modules:
  0.0 102.6 jit_solution(15347539045607218677)
XLA Ops:
  0.0 101.2 %shard_map.127 = bf16[12,4,448]{2,1,0:T(4,128)(2,1)} custom-call(s32[4,32]{1,0:T(4,128)} %bitcast.5, s32[32,48]{1,0:T(8,128)} %table_ref.1, s32[12]{0:T(128)} %context_ref.1, s32[4,32]{1,0:T(4,128)} %bitcast.6, bf16[12,4,8,576]{3,2,1,0:T(8,128)(2,1)} %queries_ref.1, bf16[12,4,576]{2,1,0:T(4,128)(2,1)} %tail_ref.1, bf16[12,4,3584]{2,1,0:T(4,128)(2,1)} %resid_ref.1, ...), custom_call_target="tpu_custom_call" | custom-call | tf_op jit(solution)/shard_map/pallas_call | solution.py:611
  101.2 1.4 %copy.15 = bf16[12,4,448]{2,1,0:T(4,128)(2,1)} copy(bf16[12,4,448]{2,1,0:T(4,128)(2,1)} %shard_map.127) | data formatting | bytes 86016

commit v4 on v3

--- a/solution.py
+++ b/solution.py
@@ -26,6 +26,8 @@
 SLABW = 512
 ROWS = 48
 RET = 384
+TILES = WIDE // 128
+CUTS = ((0, 2), (2, 2), (4, 1))
 NT = (((1,), (1,)), ((), ()))
 
 
@@ -58,7 +60,9 @@
     inv_ref,
     pos_ref,
     gain_slab,
-    h1,
+    h1_0,
+    h1_1,
+    h1_2,
     s2,
     q1,
     q2,
@@ -89,7 +93,6 @@
     krecv,
     hsend,
     hrecv,
-    qrecv,
     zsend,
     zrecv,
     tsend,
@@ -106,6 +109,7 @@
     peer_t = x * 2 + (1 - z)
 
     pending = {}
+    h1 = (h1_0, h1_1, h1_2)
 
     def finish(*names):
         for name in names or list(pending):
@@ -161,10 +165,10 @@
                 )
             for s in range(4):
                 i = (r * 4 + s) * 2 + k // 2
-                send_ref[i, 0:8, 0:576] = queries_ref[k * 3 + r, s]
-                send_ref[i, 8:16, 0:576] = queries_ref[(k + 1) * 3 + r, s]
-                send_ref[i, 0:8, 576:] = marks[0]
-                send_ref[i, 8:16, 576:] = marks[1]
+                for h in range(2):
+                    row = jnp.concatenate([queries_ref[(k + h) * 3 + r, s], marks[h]], axis=1)
+                    for w in range(TILES):
+                        send_ref[w, i, 8 * h : 8 * h + 8] = row[:, 128 * w : 128 * (w + 1)]
     for j in range(8):
 
         @pl.when(t == j)
@@ -182,48 +186,50 @@
                     return jnp.pad(block, ((0, 0), (0, WIDE - block.shape[1])))
 
                 for e in range(3):
-                    send_ref[QP + e * 2 + k // 2] = jnp.concatenate(
+                    block = jnp.concatenate(
                         [line(k, 2 * e), line(k, 2 * e + 1), line(k + 1, 2 * e), line(k + 1, 2 * e + 1)],
                         axis=0,
                     ).astype(BF16)
+                    for w in range(TILES):
+                        send_ref[w, QP + e * 2 + k // 2] = block[:, 128 * w : 128 * (w + 1)]
 
     @pl.when(g < NP)
     def _():
-        h1[g] = send_ref[g]
+        for w in range(TILES):
+            h1[w // 2][w % 2, g] = send_ref[w, g]
 
     pl.semaphore_wait(barrier, GROUPS - 1 + 7 + 16)
 
-    @pl.loop(1, GROUPS)
-    def _(d):
-        to = lax.rem(g + d, GROUPS)
-
-        @pl.when(to < NP)
-        def _():
-            pltpu.make_async_remote_copy(
-                src_ref=send_ref.at[to],
-                dst_ref=h1.at[g],
-                send_sem=hsend.at[0],
-                recv_sem=hrecv.at[0],
-                device_id={"grp": to},
-                device_id_type=MESH,
-            ).start()
-
-    def hop1_sent():
+    def hop1_sent(c):
+        chunk = pl.ds(*CUTS[c])
+
         @pl.when(g >= NP)
         def _():
-            drain(send_ref.at[pl.ds(0, NP)], hsend.at[0])
+            drain(send_ref.at[chunk, pl.ds(0, NP)], hsend.at[c])
 
         @pl.when(g < NP)
         def _():
-            drain(send_ref.at[pl.ds(0, NP - 1)], hsend.at[0])
-
-    def hop1_arrived():
-        @pl.when(g < NP)
-        def _():
-            drain(h1.at[pl.ds(0, GROUPS - 1)], hrecv.at[0])
-
-    pending["hop1_sent"] = hop1_sent
-    pending["hop1"] = hop1_arrived
+            drain(send_ref.at[chunk, pl.ds(0, NP - 1)], hsend.at[c])
+
+    for c in range(3):
+        chunk = pl.ds(*CUTS[c])
+
+        @pl.loop(1, GROUPS)
+        def _(d):
+            to = lax.rem(g + d, GROUPS)
+
+            @pl.when(to < NP)
+            def _():
+                pltpu.make_async_remote_copy(
+                    src_ref=send_ref.at[chunk, to],
+                    dst_ref=h1[c].at[:, g],
+                    send_sem=hsend.at[c],
+                    recv_sem=hrecv.at[c],
+                    device_id={"grp": to},
+                    device_id_type=MESH,
+                ).start()
+
+        pending["hop1_sent", c] = functools.partial(hop1_sent, c)
 
     place, group = iota((GROUPS, 128), 1), iota((GROUPS, 128), 0)
     inv_vec[...] = jnp.zeros((8, 128), jnp.int32)
@@ -265,69 +271,99 @@
     pending["from_left"] = to_right.wait_recv
     pending["from_right"] = to_left.wait_recv
 
-    finish("hop1")
-    @pl.when(g < NP)
-    def _():
-        kp = lax.rem(g, 2)
-        upper = iota((16, WIDE), 0) < 8
-
-        def picked(to):
-            first = h1[inv_ref[2 * kp, to]]
-            second = h1[inv_ref[2 * kp + 1, to]]
-            return jnp.where(upper, first, second)
-
-        @pl.loop(1, GROUPS)
-        def _(d):
-            to = lax.rem(g + d, GROUPS)
-            s2[to] = picked(to)
-            away = lax.rem(lax.rem(to // 2, 4) - plane + 4, 4)
-            crossing = (g < QP) & ((away == 2) | (away == 2 - turn))
-
-            @pl.when(crossing)
-            def _():
+    def hop2_sent(c):
+        @pl.when(g < NP)
+        def _():
+            drain(s2.at[pl.ds(*CUTS[c]), pl.ds(0, GROUPS - 1)], hsend.at[3 + c])
+
+    def hop2_arrived(c):
+        chunk = pl.ds(*CUTS[c])
+
+        @pl.when(g < NP)
+        def _():
+            drain(q1.at[chunk, pl.ds(0, NP - 1)], hrecv.at[3 + c])
+
+        @pl.when(g >= NP)
+        def _():
+            drain(q1.at[chunk, pl.ds(0, NP)], hrecv.at[3 + c])
+
+    for c in range(3):
+
+        @pl.when(g < NP)
+        def _():
+            chunk = pl.ds(*CUTS[c])
+            tiles = range(CUTS[c][0], CUTS[c][0] + CUTS[c][1])
+            drain(h1[c].at[:, pl.ds(0, GROUPS - 1)], hrecv.at[c])
+            kp = lax.rem(g, 2)
+            upper = iota((16, 128), 0) < 8
+
+            def picked(w, to):
+                first = h1[c][w % 2, inv_ref[2 * kp, to]]
+                second = h1[c][w % 2, inv_ref[2 * kp + 1, to]]
+                return jnp.where(upper, first, second)
+
+            @pl.loop(1, GROUPS)
+            def _(d):
+                to = lax.rem(g + d, GROUPS)
+                for w in tiles:
+                    s2[w, to] = picked(w, to)
+                away = lax.rem(lax.rem(to // 2, 4) - plane + 4, 4)
+                crossing = (g < QP) & ((away == 2) | (away == 2 - turn))
+
+                @pl.when(crossing)
+                def _():
+                    pltpu.make_async_remote_copy(
+                        src_ref=s2.at[chunk, to],
+                        dst_ref=q2.at[chunk, g],
+                        send_sem=hsend.at[3 + c],
+                        recv_sem=hrecv.at[3 + c],
+                        device_id={"grp": to, "tp": peer_t},
+                        device_id_type=MESH,
+                    ).start()
+
+                @pl.when(jnp.logical_not(crossing))
+                def _():
+                    pltpu.make_async_remote_copy(
+                        src_ref=s2.at[chunk, to],
+                        dst_ref=q1.at[chunk, g],
+                        send_sem=hsend.at[3 + c],
+                        recv_sem=hrecv.at[3 + c],
+                        device_id={"grp": to},
+                        device_id_type=MESH,
+                    ).start()
+
+            for w in tiles:
+                q1[w, g] = picked(w, g)
+
+        pending["hop2_sent", c] = functools.partial(hop2_sent, c)
+        pending["hop2", c] = functools.partial(hop2_arrived, c)
+
+    def swap_arrived(c, r):
+        drain(q2.at[pl.ds(*CUTS[c]), pl.ds(0, 8)], zrecv.at[3 * c + r])
+
+    def swap_sent(c, r):
+        drain(q2.at[pl.ds(*CUTS[c]), pl.ds(0, 8)], zsend.at[3 * c + r])
+
+    near = lax.rem(plane + turn + 4, 4)
+    far = lax.rem(plane + 2, 4)
+
+    def swap(c):
+        finish(("hop2", c))
+        for r in range(3):
+            for src, dst, at in ((q1, q2, plane), (q1, q2, near), (q2, q1, near), (q2, q1, far)):
+                part = pl.ds(8 * r + 2 * at, 2)
                 pltpu.make_async_remote_copy(
-                    src_ref=s2.at[to],
-                    dst_ref=q2.at[g],
-                    send_sem=hsend.at[1],
-                    recv_sem=qrecv.at[g // 8],
-                    device_id={"grp": to, "tp": peer_t},
+                    src_ref=src.at[pl.ds(*CUTS[c]), part],
+                    dst_ref=dst.at[pl.ds(*CUTS[c]), part],
+                    send_sem=zsend.at[3 * c + r],
+                    recv_sem=zrecv.at[3 * c + r],
+                    device_id={"tp": peer_t},
                     device_id_type=MESH,
                 ).start()
-
-            @pl.when(jnp.logical_not(crossing))
-            def _():
-                pltpu.make_async_remote_copy(
-                    src_ref=s2.at[to],
-                    dst_ref=q1.at[g],
-                    send_sem=hsend.at[1],
-                    recv_sem=qrecv.at[g // 8],
-                    device_id={"grp": to},
-                    device_id_type=MESH,
-                ).start()
-
-        q1[g] = picked(g)
-
-    def hop2_sent():
-        @pl.when(g < NP)
-        def _():
-            drain(s2.at[pl.ds(0, GROUPS - 1)], hsend.at[1])
-
-    def hop2_arrived(c):
-        count = 8 if c < 3 else EP
-
-        @pl.when(g // 8 == c)
-        def _():
-            @pl.when(g < NP)
-            def _():
-                drain(q1.at[pl.ds(0, count - 1)], qrecv.at[c])
-
-        @pl.when((g // 8 != c) | (g >= NP))
-        def _():
-            drain(q1.at[pl.ds(0, count)], qrecv.at[c])
-
-    pending["hop2_sent"] = hop2_sent
-    for c in range(4):
-        pending["hop2", c] = functools.partial(hop2_arrived, c)
+            pending["swap_sent", c, r] = functools.partial(swap_sent, c, r)
+            pending["swap", c, r] = functools.partial(swap_arrived, c, r)
+
+    swap(0)
 
     finish("from_left")
     on_right = pltpu.make_async_remote_copy(
@@ -353,56 +389,44 @@
     pending["on_left_sent"] = on_left.wait_send
     pending["across_1"] = on_right.wait_recv
     pending["across_2"] = on_left.wait_recv
-    def swap_arrived(c):
-        drain(q2.at[pl.ds(0, 8)], zrecv.at[c])
-
-    def swap_sent(c):
-        drain(q2.at[pl.ds(0, 8)], zsend.at[c])
-
-    near = lax.rem(plane + turn + 4, 4)
-    far = lax.rem(plane + 2, 4)
-    for c in range(3):
-        finish(("hop2", c))
-        for src, dst, at in ((q1, q2, plane), (q1, q2, near), (q2, q1, near), (q2, q1, far)):
-            part = pl.ds(8 * c + 2 * at, 2)
-            pltpu.make_async_remote_copy(
-                src_ref=src.at[part],
-                dst_ref=dst.at[part],
-                send_sem=zsend.at[c],
-                recv_sem=zrecv.at[c],
-                device_id={"tp": peer_t},
-                device_id_type=MESH,
-            ).start()
-        pending["swap_sent", c] = functools.partial(swap_sent, c)
-        pending["swap", c] = functools.partial(swap_arrived, c)
-    finish(("hop2", 3))
-    finish("own_keys", "across_1", "across_2")
+    swap(1)
+    swap(2)
+    finish("own_keys")
 
     nq = QP * 16
     nt = EP * 16
-    extra = q1[pl.ds(QP, EP)].reshape(nt, WIDE)
+
+    def lines(ref, first, count):
+        return jnp.concatenate(
+            [ref[w, pl.ds(first, count)].reshape(count * 16, 128) for w in range(TILES)], axis=1
+        )
+
+    extra = lines(q1, QP, EP)
 
     def keys_of(b, width):
         return jnp.concatenate([kbuf[b, j, :width] for j in range(6)], axis=1)
 
     def attend(rows, buf, tail=None):
+        count = rows.shape[0]
         lengths = rows[:, 576:577].astype(F32) * 64.0 + rows[:, 608:609].astype(F32)
-        top = jnp.full((128, 1), NEGATIVE, F32)
+        top = jnp.full((count, 1), NEGATIVE, F32)
         if tail is not None:
             top = jnp.max(tail, axis=1, keepdims=True)
-        for b in range(4):
+        for i, b in enumerate((x, left, right, across)):
+            if i == 3 and "across_1" in pending:
+                finish("across_1", "across_2")
             scores = jnp.dot(rows[:, :576], keys_of(b, 576), preferred_element_type=F32)
             scores = jnp.where(pos_ref[b * 2 + z] < lengths, scores * SCALE2, NEGATIVE)
-            buf[b] = scores
+            buf[i] = scores
             top = jnp.maximum(top, jnp.max(scores, axis=1, keepdims=True))
-        den = jnp.zeros((128, 1), F32)
-        acc = jnp.zeros((128, LATENT), F32)
+        den = jnp.zeros((count, 1), F32)
+        acc = jnp.zeros((count, LATENT), F32)
         if tail is not None:
             weight = jnp.exp2(tail - top).astype(BF16)
             den = jnp.sum(weight.astype(F32), axis=1, keepdims=True)
             acc = jnp.dot(weight, extra[:, :LATENT], preferred_element_type=F32)
-        for b in range(4):
-            weight = jnp.exp2(buf[b] - top).astype(BF16)
+        for i, b in enumerate((x, left, right, across)):
+            weight = jnp.exp2(buf[i] - top).astype(BF16)
             den = den + jnp.sum(weight.astype(F32), axis=1, keepdims=True)
             acc = acc + lax.dot_general(
                 weight, keys_of(b, LATENT), NT, preferred_element_type=F32
@@ -410,13 +434,9 @@
         return top, den, acc
 
     diagonal = iota((128, 128), 0) == iota((128, 128), 1)
-    n, m = iota((128, nt), 0), iota((128, nt), 1)
-    line = (m // 32) * 8 + m % 8
-    in_place = (line % 4 <= n // 32) & ((m // 8) % 4 == (n // 8) % 4)
-    own_top, own_den = [], []
     for c in range(3):
-        finish(("swap", c))
-        top, den, acc = attend(q2[pl.ds(8 * c, 8)].reshape(128, WIDE), sbuf.at[0])
+        finish(*[("swap", i, c) for i in range(3)])
+        top, den, acc = attend(lines(q2, 8 * c, 8), sbuf.at[:, pl.ds(128 * c, 128)])
         numer_out[c] = (acc / den).astype(BF16)
         lse = top + jnp.log2(den)
         lse_out[c] = jnp.broadcast_to(
@@ -426,32 +446,31 @@
             copy = pltpu.make_async_remote_copy(
                 src_ref=src.at[c],
                 dst_ref=dst.at[c],
-                send_sem=zsend.at[3 + 2 * c + s],
-                recv_sem=zrecv.at[3 + 2 * c + s],
+                send_sem=zsend.at[9 + 2 * c + s],
+                recv_sem=zrecv.at[9 + 2 * c + s],
                 device_id={"tp": peer_t},
                 device_id_type=MESH,
             )
             copy.start()
             pending["back_sent", c, s] = copy.wait_send
             pending["back", c, s] = copy.wait_recv
-        rows = q1[pl.ds(8 * c, 8)].reshape(128, WIDE)
-        tail = lax.dot_general(
-            rows[:, :576], extra[:, :576], NT, preferred_element_type=F32
-        )
-        tail = jnp.where(in_place & (line // 4 == c), tail * SCALE2, NEGATIVE)
-        top, den, acc = attend(rows, sbuf.at[1], tail)
-        own_top.append(top)
-        own_den.append(den)
-        acc_own[128 * c : 128 * (c + 1)] = acc
+    rows = lines(q1, 0, QP)
+    n, m = iota((nq, nt), 0), iota((nq, nt), 1)
+    line = (m // 32) * 8 + m % 8
+    seen = (line // 4 == n // 128) & (line % 4 <= (n // 32) % 4)
+    seen = seen & ((m // 8) % 4 == (n // 8) % 4)
+    tail = lax.dot_general(rows[:, :576], extra[:, :576], NT, preferred_element_type=F32)
+    tail = jnp.where(seen, tail * SCALE2, NEGATIVE)
+    own_top, own_den, acc_own[...] = attend(rows, sbuf, tail)
     finish("weights")
     for c in range(3):
         finish(("back", c, 0), ("back", c, 1))
         at = slice(128 * c, 128 * (c + 1))
         lse = jnp.sum(jnp.where(diagonal, lse_in[c, 0:1, :], 0.0), axis=1, keepdims=True)
-        both = jnp.maximum(own_top[c], lse)
-        mine = jnp.exp2(own_top[c] - both)
+        both = jnp.maximum(own_top[at], lse)
+        mine = jnp.exp2(own_top[at] - both)
         theirs = jnp.exp2(lse - both)
-        scaled = 1.0 / (own_den[c] * mine + theirs)
+        scaled = 1.0 / (own_den[at] * mine + theirs)
         latent[at] = (
             acc_own[at] * (mine * scaled) + numer_in[c].astype(F32) * (theirs * scaled)
         ).astype(BF16)
@@ -569,15 +588,15 @@
         pltpu.make_async_remote_copy(
             src_ref=sback.at[to],
             dst_ref=rback.at[g],
-            send_sem=hsend.at[2],
-            recv_sem=hrecv.at[2],
+            send_sem=hsend.at[6],
+            recv_sem=hrecv.at[6],
             device_id={"grp": to},
             device_id_type=MESH,
         ).start()
 
     rback[g] = answer(g)
-    pending["return_sent"] = lambda: drain(sback.at[pl.ds(0, GROUPS - 1)], hsend.at[2])
-    pending["return"] = lambda: drain(rback.at[pl.ds(0, GROUPS - 1)], hrecv.at[2])
+    pending["return_sent"] = lambda: drain(sback.at[pl.ds(0, GROUPS - 1)], hsend.at[6])
+    pending["return"] = lambda: drain(rback.at[pl.ds(0, GROUPS - 1)], hrecv.at[6])
     finish("return")
     for k in range(4):
         block = rback[reads_ref[k, g]].astype(F32)
@@ -614,18 +633,20 @@
         in_specs=[smem] * 3 + [vmem] * 5 + [anym] * 6,
         out_specs=vmem,
         scratch_shapes=[
-            pltpu.VMEM((NP, 16, WIDE), BF16),
+            pltpu.VMEM((TILES, NP, 16, 128), BF16),
             pltpu.VMEM((8, 128), jnp.int32),
             pltpu.SMEM((8, 128), jnp.int32),
             pltpu.VMEM((8, 1, 768), F32),
             pltpu.VMEM((1, SLABW), F32),
-            pltpu.VMEM((GROUPS, 16, WIDE), BF16),
-            pltpu.VMEM((GROUPS, 16, WIDE), BF16),
-            pltpu.VMEM((NP, 16, WIDE), BF16),
-            pltpu.VMEM((QP, 16, WIDE), BF16),
+            pltpu.VMEM((2, GROUPS, 16, 128), BF16),
+            pltpu.VMEM((2, GROUPS, 16, 128), BF16),
+            pltpu.VMEM((1, GROUPS, 16, 128), BF16),
+            pltpu.VMEM((TILES, GROUPS, 16, 128), BF16),
+            pltpu.VMEM((TILES, NP, 16, 128), BF16),
+            pltpu.VMEM((TILES, QP, 16, 128), BF16),
             pltpu.VMEM((4, 6, 576, 128), BF16),
             pltpu.VMEM((nq, LATENT), F32),
-            pltpu.VMEM((2, 4, 128, 768), F32),
+            pltpu.VMEM((4, nq, 768), F32),
             pltpu.VMEM((3, 128, LATENT), BF16),
             pltpu.VMEM((3, 128, LATENT), BF16),
             pltpu.VMEM((3, 8, 128), F32),
@@ -648,11 +669,10 @@
             dma((7,)),
             dma((4,)),
             dma((4,)),
-            dma((3,)),
-            dma((3,)),
-            dma((4,)),
-            dma((9,)),
-            dma((9,)),
+            dma((7,)),
+            dma((7,)),
+            dma((15,)),
+            dma((15,)),
             dma((3,)),
             dma((3,)),
         ],

time: 103 us -> 99.9 us (0.970)
  Pallas kernels: 101 us -> 98 us
    pallas_call x1, Pallas kernels: 101 us -> 98 us  [on_device(): pl.pallas_call(kernel, out_shape=jax.ShapeDtypeStruct((12, 4, SLAB), BF16...]
where the time goes in v4:
time: 99.9 us; the launch traced here: 99.5 us
  Pallas kernels  98 us (98%)
  local copies, waits for them, and re-layouts  1.44 us (1%)
    pallas_call x1, Pallas kernels, on_device(): pl.pallas_call(kernel, out_shape=jax.ShapeDtypeStruct((12, 4, SLAB), BF16...  98 us

profile of v4, /device:TPU:1, one launch (start us, length us, event | category | flops | bytes accessed | tf_op | source)
XLA Modules:
  0.0 99.5 jit_solution(14470919436718106833)
XLA Ops:
  0.0 98.0 %shard_map.127 = bf16[12,4,448]{2,1,0:T(4,128)(2,1)} custom-call(s32[4,32]{1,0:T(4,128)} %bitcast.5, s32[32,48]{1,0:T(8,128)} %table_ref.1, s32[12]{0:T(128)} %context_ref.1, s32[4,32]{1,0:T(4,128)} %bitcast.6, bf16[12,4,8,576]{3,2,1,0:T(8,128)(2,1)} %queries_ref.1, bf16[12,4,576]{2,1,0:T(4,128)(2,1)} %tail_ref.1, bf16[12,4,3584]{2,1,0:T(4,128)(2,1)} %resid_ref.1, ...), custom_call_target="tpu_custom_call" | custom-call | tf_op jit(solution)/shard_map/pallas_call | solution.py:630
  98.0 1.4 %copy.15 = bf16[12,4,448]{2,1,0:T(4,128)(2,1)} copy(bf16[12,4,448]{2,1,0:T(4,128)(2,1)} %shard_map.127) | data formatting | bytes 86016

commit v5 on v4

--- a/solution.py
+++ b/solution.py
@@ -88,6 +88,10 @@
     fin,
     sback,
     rback,
+    home_out,
+    home_mid,
+    home_next,
+    home_in,
     wsem,
     ksend,
     krecv,
@@ -97,6 +101,8 @@
     zrecv,
     tsend,
     trecv,
+    bsend,
+    brecv,
 ):
     g = lax.axis_index("grp")
     t = lax.axis_index("tp")
@@ -362,8 +368,6 @@
                 ).start()
             pending["swap_sent", c, r] = functools.partial(swap_sent, c, r)
             pending["swap", c, r] = functools.partial(swap_arrived, c, r)
-
-    swap(0)
 
     finish("from_left")
     on_right = pltpu.make_async_remote_copy(
@@ -389,6 +393,7 @@
     pending["on_left_sent"] = on_left.wait_send
     pending["across_1"] = on_right.wait_recv
     pending["across_2"] = on_left.wait_recv
+    swap(0)
     swap(1)
     swap(2)
     finish("own_keys")
@@ -534,6 +539,63 @@
     agout[...] = packed
     spread(lambda to: agout, ag, 1)
     ag[t] = packed
+
+    o, m = iota((64, ROWS), 0), iota((64, ROWS), 1)
+
+    def placed(chosen, columns):
+        return jnp.dot(
+            jnp.where((o // 16 == m // 12) & chosen, 1.0, 0.0).astype(BF16),
+            columns,
+            preferred_element_type=F32,
+        )
+
+    rounded = hidden.astype(BF16)
+    wide = placed(o % 16 == m % 12, rounded[:, :RET])
+    rest = [
+        placed(o % 16 - 12 + 4 * r == m % 12, rounded[:, RET:SLAB]) for r in range(3)
+    ]
+    rest = jnp.concatenate(rest + [jnp.zeros((64, RET - 192), F32)], axis=1)
+    lower = iota((64, RET), 0) % 16 >= 12
+    block = jnp.where(lower, rest, wide).astype(BF16)
+    for i in range(12):
+        home_out[i] = block[16 * (i // 3) : 16 * (i // 3) + 16, 128 * (i % 3) : 128 * (i % 3 + 1)]
+        copy = pltpu.make_async_remote_copy(
+            src_ref=home_out.at[i],
+            dst_ref=home_mid.at[g],
+            send_sem=bsend.at[i],
+            recv_sem=brecv.at[0],
+            device_id={"grp": i},
+            device_id_type=MESH,
+        )
+
+        @pl.when(g != i)
+        def _():
+            copy.start()
+
+        @pl.when(g == i)
+        def _():
+            home_mid[g] = home_out[i]
+
+    def home_sent():
+        for i in range(12):
+
+            @pl.when(g != i)
+            def _():
+                drain(home_out.at[i], bsend.at[i])
+
+        @pl.when(g < 12)
+        def _():
+            drain(home_next.at[pl.ds(0, GROUPS - 1)], bsend.at[12])
+
+    def home_arrived():
+        @pl.when(g < 12)
+        def _():
+            drain(home_in.at[pl.ds(0, 11)], brecv.at[1])
+
+        @pl.when(g >= 12)
+        def _():
+            drain(home_in.at[pl.ds(0, 12)], brecv.at[1])
+
     finish(("spread", 1))
     total = jnp.zeros((ROWS, 1), F32)
     gate = jnp.zeros((ROWS, 128), F32)
@@ -550,30 +612,8 @@
     gate = gate * factor
     upward = upward * factor
     active = (gate / (1.0 + jnp.exp(-gate)) * upward).astype(BF16)
-    slabs(active, wdown, mix.at[1])
-    spread(lambda to: mix.at[1, to], rs2, 2)
-    rs2[t] = mix[1, t]
-    finish(("spread", 2))
-    for j in range(8):
-        hidden = hidden + rs2[j].astype(F32)
-
-    o, m = iota((64, ROWS), 0), iota((64, ROWS), 1)
-    result = hidden.astype(BF16)
-
-    def placed(chosen, columns):
-        return jnp.dot(
-            jnp.where((o // 16 == m // 12) & chosen, 1.0, 0.0).astype(BF16),
-            columns,
-            preferred_element_type=F32,
-        )
-
-    wide = placed(o % 16 == m % 12, result[:, :RET])
-    rest = [
-        placed(o % 16 - 12 + 4 * r == m % 12, result[:, RET:SLAB]) for r in range(3)
-    ]
-    rest = jnp.concatenate(rest + [jnp.zeros((64, RET - 192), F32)], axis=1)
-    lower = iota((64, RET), 0) % 16 >= 12
-    fin[...] = jnp.where(lower, rest, wide).astype(BF16).reshape(4, 16, RET)
+
+    fin[...] = placed(o % 16 == m % 12, active).astype(BF16).reshape(4, 16, 128)
 
     def answer(to):
         slot = jnp.where(reads_ref[3, to] == g, 3, 0)
@@ -597,12 +637,55 @@
     rback[g] = answer(g)
     pending["return_sent"] = lambda: drain(sback.at[pl.ds(0, GROUPS - 1)], hsend.at[6])
     pending["return"] = lambda: drain(rback.at[pl.ds(0, GROUPS - 1)], hrecv.at[6])
+
+    @pl.when(g < 12)
+    def _():
+        drain(home_mid.at[pl.ds(0, GROUPS - 1)], brecv.at[0])
+        k = g // 3
+
+        @pl.loop(1, GROUPS)
+        def _(d):
+            to = lax.rem(g + d, GROUPS)
+            home_next[to] = home_mid[reads_ref[k, to]]
+            pltpu.make_async_remote_copy(
+                src_ref=home_next.at[to],
+                dst_ref=home_in.at[g],
+                send_sem=bsend.at[12],
+                recv_sem=brecv.at[1],
+                device_id={"grp": to},
+                device_id_type=MESH,
+            ).start()
+
+        home_in[g] = home_mid[reads_ref[k, g]]
+
+    pending["home_sent"] = home_sent
+    pending["home"] = home_arrived
     finish("return")
+    o, m = iota((ROWS, 64), 0), iota((ROWS, 64), 1)
+    blocks = jnp.concatenate([rback[reads_ref[k, g]] for k in range(4)], axis=0)
+    active = jnp.dot(
+        jnp.where((o // 12 == m // 16) & (o % 12 == m % 16), 1.0, 0.0).astype(BF16),
+        blocks,
+        preferred_element_type=F32,
+    ).astype(BF16)
+    slabs(active, wdown, mix.at[1])
+    spread(lambda to: mix.at[1, to], rs2, 2)
+    rs2[t] = mix[1, t]
+    finish("home")
+    finish(("spread", 2))
+    summed = rs2[0].astype(F32)
+    for j in range(1, 8):
+        summed = summed + rs2[j].astype(F32)
     for k in range(4):
-        block = rback[reads_ref[k, g]].astype(F32)
+        block = jnp.concatenate([home_in[3 * k + j] for j in range(3)], axis=1).astype(F32)
         for r in range(3):
-            out_ref[3 * k + r, :, :RET] = block[4 * r : 4 * r + 4].astype(BF16)
-            out_ref[3 * k + r, :, RET:] = block[12:, 64 * r : 64 * r + 64].astype(BF16)
+            at = slice(12 * k + 4 * r, 12 * k + 4 * r + 4)
+            out_ref[3 * k + r, :, :RET] = (
+                summed[at, :RET] + block[4 * r : 4 * r + 4]
+            ).astype(BF16)
+            out_ref[3 * k + r, :, RET:] = (
+                summed[at, RET:SLAB] + block[12:, 64 * r : 64 * r + 64]
+            ).astype(BF16)
 
     finish()
 
@@ -663,9 +746,13 @@
             pltpu.VMEM((ROWS, SLABW), BF16),
             pltpu.VMEM((8, ROWS, SLABW), BF16),
             pltpu.VMEM((8, ROWS, SLABW), BF16),
-            pltpu.VMEM((4, 16, RET), BF16),
-            pltpu.VMEM((GROUPS, 16, RET), BF16),
-            pltpu.VMEM((GROUPS, 16, RET), BF16),
+            pltpu.VMEM((4, 16, 128), BF16),
+            pltpu.VMEM((GROUPS, 16, 128), BF16),
+            pltpu.VMEM((GROUPS, 16, 128), BF16),
+            pltpu.VMEM((12, 16, 128), BF16),
+            pltpu.VMEM((GROUPS, 16, 128), BF16),
+            pltpu.VMEM((GROUPS, 16, 128), BF16),
+            pltpu.VMEM((12, 16, 128), BF16),
             dma((7,)),
             dma((4,)),
             dma((4,)),
@@ -675,6 +762,8 @@
             dma((15,)),
             dma((3,)),
             dma((3,)),
+            dma((13,)),
+            dma((2,)),
         ],
         compiler_params=pltpu.CompilerParams(
             collective_id=0, has_side_effects=True, vmem_limit_bytes=56 * 1024 * 1024

time: 99.9 us -> 96.7 us (0.968)
  Pallas kernels: 98 us -> 95.1 us
    pallas_call x1, Pallas kernels: 98 us -> 95.1 us  [on_device(): pl.pallas_call(kernel, out_shape=jax.ShapeDtypeStruct((12, 4, SLAB), BF16...]
where the time goes in v5:
time: 96.7 us; the launch traced here: 96.5 us
  Pallas kernels  95.1 us (98%)
  local copies, waits for them, and re-layouts  1.44 us (1%)
    pallas_call x1, Pallas kernels, on_device(): pl.pallas_call(kernel, out_shape=jax.ShapeDtypeStruct((12, 4, SLAB), BF16...  95.1 us

profile of v5, /device:TPU:1, one launch (start us, length us, event | category | flops | bytes accessed | tf_op | source)
XLA Modules:
  0.0 96.5 jit_solution(10085101661888651558)
XLA Ops:
  0.0 95.1 %shard_map.127 = bf16[12,4,448]{2,1,0:T(4,128)(2,1)} custom-call(s32[4,32]{1,0:T(4,128)} %bitcast.5, s32[32,48]{1,0:T(8,128)} %table_ref.1, s32[12]{0:T(128)} %context_ref.1, s32[4,32]{1,0:T(4,128)} %bitcast.6, bf16[12,4,8,576]{3,2,1,0:T(8,128)(2,1)} %queries_ref.1, bf16[12,4,576]{2,1,0:T(4,128)(2,1)} %tail_ref.1, bf16[12,4,3584]{2,1,0:T(4,128)(2,1)} %resid_ref.1, ...), custom_call_target="tpu_custom_call" | custom-call | tf_op jit(solution)/shard_map/pallas_call | solution.py:713
  95.1 1.4 %copy.15 = bf16[12,4,448]{2,1,0:T(4,128)(2,1)} copy(bf16[12,4,448]{2,1,0:T(4,128)(2,1)} %shard_map.127) | data formatting | bytes 86016

commit v6 on v5

--- a/solution.py
+++ b/solution.py
@@ -28,6 +28,7 @@
 RET = 384
 TILES = WIDE // 128
 CUTS = ((0, 2), (2, 2), (4, 1))
+HALF = 192
 NT = (((1,), (1,)), ((), ()))
 
 
@@ -170,11 +171,13 @@
                     jnp.where(half, length // 64, length % 64).astype(F32).astype(BF16)
                 )
             for s in range(4):
-                i = (r * 4 + s) * 2 + k // 2
                 for h in range(2):
                     row = jnp.concatenate([queries_ref[(k + h) * 3 + r, s], marks[h]], axis=1)
                     for w in range(TILES):
-                        send_ref[w, i, 8 * h : 8 * h + 8] = row[:, 128 * w : 128 * (w + 1)]
+                        u = (r * 4 + s) * TILES + w
+                        send_ref[k + u % 2, u // 2, 8 * h : 8 * h + 8] = row[
+                            :, 128 * w : 128 * (w + 1)
+                        ]
     for j in range(8):
 
         @pl.when(t == j)
@@ -197,7 +200,9 @@
                         axis=0,
                     ).astype(BF16)
                     for w in range(TILES):
-                        send_ref[w, QP + e * 2 + k // 2] = block[:, 128 * w : 128 * (w + 1)]
+                        send_ref[4, (e * 2 + k // 2) * TILES + w] = block[
+                            :, 128 * w : 128 * (w + 1)
+                        ]
 
     @pl.when(g < NP)
     def _():
@@ -282,16 +287,21 @@
         def _():
             drain(s2.at[pl.ds(*CUTS[c]), pl.ds(0, GROUPS - 1)], hsend.at[3 + c])
 
+    near = lax.rem(plane + turn + 4, 4)
+    far = lax.rem(plane + 2, 4)
+
     def hop2_arrived(c):
         chunk = pl.ds(*CUTS[c])
-
-        @pl.when(g < NP)
-        def _():
-            drain(q1.at[chunk, pl.ds(0, NP - 1)], hrecv.at[3 + c])
-
-        @pl.when(g >= NP)
-        def _():
-            drain(q1.at[chunk, pl.ds(0, NP)], hrecv.at[3 + c])
+        count = jnp.int32(NP)
+        if c < 2:
+            count = GROUPS - 2 * jnp.where((plane == 3) | (far == 3), 1, 0)
+            count = count - 4 * jnp.where(near == 3, 1, 0)
+        count = count - jnp.where(g < NP, 1, 0)
+        for n in range(GROUPS - 5, GROUPS + 1):
+
+            @pl.when(count == n)
+            def _():
+                drain(q1.at[chunk, pl.ds(0, n)], hrecv.at[3 + c])
 
     for c in range(3):
 
@@ -300,7 +310,7 @@
             chunk = pl.ds(*CUTS[c])
             tiles = range(CUTS[c][0], CUTS[c][0] + CUTS[c][1])
             drain(h1[c].at[:, pl.ds(0, GROUPS - 1)], hrecv.at[c])
-            kp = lax.rem(g, 2)
+            kp = (0, 1, lax.rem(g // TILES, 2))[c]
             upper = iota((16, 128), 0) < 8
 
             def picked(w, to):
@@ -314,29 +324,23 @@
                 for w in tiles:
                     s2[w, to] = picked(w, to)
                 away = lax.rem(lax.rem(to // 2, 4) - plane + 4, 4)
-                crossing = (g < QP) & ((away == 2) | (away == 2 - turn))
-
-                @pl.when(crossing)
-                def _():
+                crossing = (away == 2) | (away == 2 - turn)
+
+                def hop2(dst, device):
                     pltpu.make_async_remote_copy(
                         src_ref=s2.at[chunk, to],
-                        dst_ref=q2.at[chunk, g],
+                        dst_ref=dst.at[chunk, g],
                         send_sem=hsend.at[3 + c],
                         recv_sem=hrecv.at[3 + c],
-                        device_id={"grp": to, "tp": peer_t},
+                        device_id=device,
                         device_id_type=MESH,
                     ).start()
 
-                @pl.when(jnp.logical_not(crossing))
-                def _():
-                    pltpu.make_async_remote_copy(
-                        src_ref=s2.at[chunk, to],
-                        dst_ref=q1.at[chunk, g],
-                        send_sem=hsend.at[3 + c],
-                        recv_sem=hrecv.at[3 + c],
-                        device_id={"grp": to},
-                        device_id_type=MESH,
-                    ).start()
+                if c == 2:
+                    hop2(q1, {"grp": to})
+                else:
+                    pl.when(crossing)(lambda: hop2(q2, {"grp": to, "tp": peer_t}))
+                    pl.when(jnp.logical_not(crossing))(lambda: hop2(q1, {"grp": to}))
 
             for w in tiles:
                 q1[w, g] = picked(w, g)
@@ -344,30 +348,27 @@
         pending["hop2_sent", c] = functools.partial(hop2_sent, c)
         pending["hop2", c] = functools.partial(hop2_arrived, c)
 
-    def swap_arrived(c, r):
-        drain(q2.at[pl.ds(*CUTS[c]), pl.ds(0, 8)], zrecv.at[3 * c + r])
-
-    def swap_sent(c, r):
-        drain(q2.at[pl.ds(*CUTS[c]), pl.ds(0, 8)], zsend.at[3 * c + r])
-
-    near = lax.rem(plane + turn + 4, 4)
-    far = lax.rem(plane + 2, 4)
+    def swap_arrived(c):
+        drain(q2.at[pl.ds(*CUTS[c])], zrecv.at[c])
+
+    def swap_sent(c):
+        drain(q2.at[pl.ds(*CUTS[c])], zsend.at[c])
 
     def swap(c):
         finish(("hop2", c))
-        for r in range(3):
-            for src, dst, at in ((q1, q2, plane), (q1, q2, near), (q2, q1, near), (q2, q1, far)):
-                part = pl.ds(8 * r + 2 * at, 2)
+        for src, dst, at in ((q1, q2, plane), (q1, q2, near), (q2, q1, near), (q2, q1, far)):
+            for y in range(4):
+                part = pl.ds(8 * y + 2 * at, 2)
                 pltpu.make_async_remote_copy(
                     src_ref=src.at[pl.ds(*CUTS[c]), part],
                     dst_ref=dst.at[pl.ds(*CUTS[c]), part],
-                    send_sem=zsend.at[3 * c + r],
-                    recv_sem=zrecv.at[3 * c + r],
+                    send_sem=zsend.at[c],
+                    recv_sem=zrecv.at[c],
                     device_id={"tp": peer_t},
                     device_id_type=MESH,
                 ).start()
-            pending["swap_sent", c, r] = functools.partial(swap_sent, c, r)
-            pending["swap", c, r] = functools.partial(swap_arrived, c, r)
+        pending["swap_sent", c] = functools.partial(swap_sent, c)
+        pending["swap", c] = functools.partial(swap_arrived, c)
 
     finish("from_left")
     on_right = pltpu.make_async_remote_copy(
@@ -395,18 +396,19 @@
     pending["across_2"] = on_left.wait_recv
     swap(0)
     swap(1)
-    swap(2)
     finish("own_keys")
 
     nq = QP * 16
     nt = EP * 16
 
-    def lines(ref, first, count):
-        return jnp.concatenate(
-            [ref[w, pl.ds(first, count)].reshape(count * 16, 128) for w in range(TILES)], axis=1
-        )
-
-    extra = lines(q1, QP, EP)
+    def lines(ref, slot, step, count):
+        pieces = []
+        for i in range(count):
+            units = [i * TILES + w for w in range(TILES)]
+            pieces.append(
+                jnp.concatenate([ref[slot + u % step, u // step] for u in units], axis=1)
+            )
+        return jnp.concatenate(pieces, axis=0)
 
     def keys_of(b, width):
         return jnp.concatenate([kbuf[b, j, :width] for j in range(6)], axis=1)
@@ -438,44 +440,53 @@
             )
         return top, den, acc
 
-    diagonal = iota((128, 128), 0) == iota((128, 128), 1)
-    for c in range(3):
-        finish(*[("swap", i, c) for i in range(3)])
-        top, den, acc = attend(lines(q2, 8 * c, 8), sbuf.at[:, pl.ds(128 * c, 128)])
+    diagonal = iota((HALF, HALF), 0) == iota((HALF, HALF), 1)
+    n, m = iota((HALF, nt), 0), iota((HALF, nt), 1)
+    line = (m // 32) * 8 + m % 8
+    in_place = (line // 4 == n // 64) & (line % 4 <= (n // 16) % 4)
+    own_top, own_den = [], []
+    for c in range(2):
+        finish(("swap", c))
+        top, den, acc = attend(lines(q2, 2 * c, 2, 12), sbuf.at[0])
         numer_out[c] = (acc / den).astype(BF16)
         lse = top + jnp.log2(den)
         lse_out[c] = jnp.broadcast_to(
-            jnp.sum(jnp.where(diagonal, lse, 0.0), axis=0, keepdims=True), (8, 128)
+            jnp.sum(jnp.where(diagonal, lse, 0.0), axis=0, keepdims=True), (8, HALF)
         )
         for s, (src, dst) in enumerate([(numer_out, numer_in), (lse_out, lse_in)]):
             copy = pltpu.make_async_remote_copy(
                 src_ref=src.at[c],
                 dst_ref=dst.at[c],
-                send_sem=zsend.at[9 + 2 * c + s],
-                recv_sem=zrecv.at[9 + 2 * c + s],
+                send_sem=zsend.at[2 + 2 * c + s],
+                recv_sem=zrecv.at[2 + 2 * c + s],
                 device_id={"tp": peer_t},
                 device_id_type=MESH,
             )
             copy.start()
             pending["back_sent", c, s] = copy.wait_send
             pending["back", c, s] = copy.wait_recv
-    rows = lines(q1, 0, QP)
-    n, m = iota((nq, nt), 0), iota((nq, nt), 1)
-    line = (m // 32) * 8 + m % 8
-    seen = (line // 4 == n // 128) & (line % 4 <= (n // 32) % 4)
-    seen = seen & ((m // 8) % 4 == (n // 8) % 4)
-    tail = lax.dot_general(rows[:, :576], extra[:, :576], NT, preferred_element_type=F32)
-    tail = jnp.where(seen, tail * SCALE2, NEGATIVE)
-    own_top, own_den, acc_own[...] = attend(rows, sbuf, tail)
+        if c == 0:
+            finish(("hop2", 2))
+            extra = lines(q1, 4, 1, EP)
+        rows = lines(q1, 2 * c, 2, 12)
+        tail = lax.dot_general(
+            rows[:, :576], extra[:, :576], NT, preferred_element_type=F32
+        )
+        seen = in_place & ((m // 8) % 4 == 2 * c + (n // 8) % 2)
+        tail = jnp.where(seen, tail * SCALE2, NEGATIVE)
+        top, den, acc = attend(rows, sbuf.at[1], tail)
+        own_top.append(top)
+        own_den.append(den)
+        acc_own[HALF * c : HALF * (c + 1)] = acc
     finish("weights")
-    for c in range(3):
+    for c in range(2):
         finish(("back", c, 0), ("back", c, 1))
-        at = slice(128 * c, 128 * (c + 1))
+        at = slice(HALF * c, HALF * (c + 1))
         lse = jnp.sum(jnp.where(diagonal, lse_in[c, 0:1, :], 0.0), axis=1, keepdims=True)
-        both = jnp.maximum(own_top[at], lse)
-        mine = jnp.exp2(own_top[at] - both)
+        both = jnp.maximum(own_top[c], lse)
+        mine = jnp.exp2(own_top[c] - both)
         theirs = jnp.exp2(lse - both)
-        scaled = 1.0 / (own_den[at] * mine + theirs)
+        scaled = 1.0 / (own_den[c] * mine + theirs)
         latent[at] = (
             acc_own[at] * (mine * scaled) + numer_in[c].astype(F32) * (theirs * scaled)
         ).astype(BF16)
@@ -485,7 +496,8 @@
         value = jnp.dot(latent[...], wuv[h], preferred_element_type=F32)
         flatm[:, h * 128 : (h + 1) * 128] = jnp.where(head_of == h, value, 0.0).astype(BF16)
     o, n = iota((ROWS, nq), 0), iota((ROWS, nq), 1)
-    chosen = ((n // 32) == o % 12) & ((n // 8) % 4 == o // 12)
+    chosen = (n % HALF) // 16 == o % 12
+    chosen = chosen & ((n // HALF) * 2 + (n // 8) % 2 == o // 12)
     flat = jnp.dot(
         jnp.where(chosen, 1.0, 0.0).astype(BF16), flatm[...], preferred_element_type=F32
     ).astype(BF16)
@@ -725,15 +737,15 @@
             pltpu.VMEM((2, GROUPS, 16, 128), BF16),
             pltpu.VMEM((1, GROUPS, 16, 128), BF16),
             pltpu.VMEM((TILES, GROUPS, 16, 128), BF16),
-            pltpu.VMEM((TILES, NP, 16, 128), BF16),
-            pltpu.VMEM((TILES, QP, 16, 128), BF16),
+            pltpu.VMEM((TILES, GROUPS, 16, 128), BF16),
+            pltpu.VMEM((4, GROUPS, 16, 128), BF16),
             pltpu.VMEM((4, 6, 576, 128), BF16),
             pltpu.VMEM((nq, LATENT), F32),
-            pltpu.VMEM((4, nq, 768), F32),
-            pltpu.VMEM((3, 128, LATENT), BF16),
-            pltpu.VMEM((3, 128, LATENT), BF16),
-            pltpu.VMEM((3, 8, 128), F32),
-            pltpu.VMEM((3, 8, 128), F32),
+            pltpu.VMEM((2, 4, HALF, 768), F32),
+            pltpu.VMEM((2, HALF, LATENT), BF16),
+            pltpu.VMEM((2, HALF, LATENT), BF16),
+            pltpu.VMEM((2, 8, HALF), F32),
+            pltpu.VMEM((2, 8, HALF), F32),
             pltpu.VMEM((nq, LATENT), BF16),
             pltpu.VMEM((nq, 1024), BF16),
             pltpu.VMEM((8, 512, 128), BF16),
@@ -758,8 +770,8 @@
             dma((4,)),
             dma((7,)),
             dma((7,)),
-            dma((15,)),
-            dma((15,)),
+            dma((6,)),
+            dma((6,)),
             dma((3,)),
             dma((3,)),
             dma((13,)),

time: 96.7 us -> 95.5 us (0.988)
  Pallas kernels: 95.1 us -> 93.9 us
    pallas_call x1, Pallas kernels: 95.1 us -> 93.9 us  [on_device(): pl.pallas_call(kernel, out_shape=jax.ShapeDtypeStruct((12, 4, SLAB), BF16...]
where the time goes in v6:
time: 95.5 us; the launch traced here: 95.4 us
  Pallas kernels  93.9 us (98%)
  local copies, waits for them, and re-layouts  1.44 us (2%)
    pallas_call x1, Pallas kernels, on_device(): pl.pallas_call(kernel, out_shape=jax.ShapeDtypeStruct((12, 4, SLAB), BF16...  93.9 us

profile of v6, /device:TPU:1, one launch (start us, length us, event | category | flops | bytes accessed | tf_op | source)
XLA Modules:
  0.0 95.4 jit_solution(9683181852248295921)
XLA Ops:
  0.0 93.9 %shard_map.127 = bf16[12,4,448]{2,1,0:T(4,128)(2,1)} custom-call(s32[4,32]{1,0:T(4,128)} %bitcast.5, s32[32,48]{1,0:T(8,128)} %table_ref.1, s32[12]{0:T(128)} %context_ref.1, s32[4,32]{1,0:T(4,128)} %bitcast.6, bf16[12,4,8,576]{3,2,1,0:T(8,128)(2,1)} %queries_ref.1, bf16[12,4,576]{2,1,0:T(4,128)(2,1)} %tail_ref.1, bf16[12,4,3584]{2,1,0:T(4,128)(2,1)} %resid_ref.1, ...), custom_call_target="tpu_custom_call" | custom-call | tf_op jit(solution)/shard_map/pallas_call | solution.py:725
  93.9 1.4 %copy.15 = bf16[12,4,448]{2,1,0:T(4,128)(2,1)} copy(bf16[12,4,448]{2,1,0:T(4,128)(2,1)} %shard_map.127) | data formatting | bytes 86016

commit v7 on v6

--- a/solution.py
+++ b/solution.py
@@ -222,7 +222,7 @@
         def _():
             drain(send_ref.at[chunk, pl.ds(0, NP - 1)], hsend.at[c])
 
-    for c in range(3):
+    def hop1(c):
         chunk = pl.ds(*CUTS[c])
 
         @pl.loop(1, GROUPS)
@@ -241,6 +241,9 @@
                 ).start()
 
         pending["hop1_sent", c] = functools.partial(hop1_sent, c)
+
+    hop1(0)
+    hop1(1)
 
     place, group = iota((GROUPS, 128), 1), iota((GROUPS, 128), 0)
     inv_vec[...] = jnp.zeros((8, 128), jnp.int32)
@@ -303,7 +306,7 @@
             def _():
                 drain(q1.at[chunk, pl.ds(0, n)], hrecv.at[3 + c])
 
-    for c in range(3):
+    def route(c):
 
         @pl.when(g < NP)
         def _():
@@ -347,6 +350,9 @@
 
         pending["hop2_sent", c] = functools.partial(hop2_sent, c)
         pending["hop2", c] = functools.partial(hop2_arrived, c)
+
+    route(0)
+    route(1)
 
     def swap_arrived(c):
         drain(q2.at[pl.ds(*CUTS[c])], zrecv.at[c])
@@ -395,6 +401,7 @@
     pending["across_1"] = on_right.wait_recv
     pending["across_2"] = on_left.wait_recv
     swap(0)
+    hop1(2)
     swap(1)
     finish("own_keys")
 
@@ -466,8 +473,10 @@
             pending["back_sent", c, s] = copy.wait_send
             pending["back", c, s] = copy.wait_recv
         if c == 0:
-            finish(("hop2", 2))
-            extra = lines(q1, 4, 1, EP)
+            route(2)
+    finish(("hop2", 2))
+    extra = lines(q1, 4, 1, EP)
+    for c in range(2):
         rows = lines(q1, 2 * c, 2, 12)
         tail = lax.dot_general(
             rows[:, :576], extra[:, :576], NT, preferred_element_type=F32

time: 95.5 us -> 101 us (1.058)
  Pallas kernels: 93.9 us -> 99.2 us
    pallas_call x1, Pallas kernels: 93.9 us -> 99.2 us  [on_device(): pl.pallas_call(kernel, out_shape=jax.ShapeDtypeStruct((12, 4, SLAB), BF16...]
where the time goes in v7:
time: 101 us
  Pallas kernels  99.2 us (98%)
  local copies, waits for them, and re-layouts  1.44 us (1%)
    pallas_call x1, Pallas kernels, on_device(): pl.pallas_call(kernel, out_shape=jax.ShapeDtypeStruct((12, 4, SLAB), BF16...  99.2 us

profile of v7, /device:TPU:1, one launch (start us, length us, event | category | flops | bytes accessed | tf_op | source)
XLA Modules:
  0.0 100.7 jit_solution(13258681853774517839)
XLA Ops:
  0.0 99.2 %shard_map.127 = bf16[12,4,448]{2,1,0:T(4,128)(2,1)} custom-call(s32[4,32]{1,0:T(4,128)} %bitcast.5, s32[32,48]{1,0:T(8,128)} %table_ref.1, s32[12]{0:T(128)} %context_ref.1, s32[4,32]{1,0:T(4,128)} %bitcast.6, bf16[12,4,8,576]{3,2,1,0:T(8,128)(2,1)} %queries_ref.1, bf16[12,4,576]{2,1,0:T(4,128)(2,1)} %tail_ref.1, bf16[12,4,3584]{2,1,0:T(4,128)(2,1)} %resid_ref.1, ...), custom_call_target="tpu_custom_call" | custom-call | tf_op jit(solution)/shard_map/pallas_call | solution.py:734
  99.2 1.4 %copy.15 = bf16[12,4,448]{2,1,0:T(4,128)(2,1)} copy(bf16[12,4,448]{2,1,0:T(4,128)(2,1)} %shard_map.127) | data formatting | bytes 86016

commit v8 on v7

--- a/solution.py
+++ b/solution.py
@@ -244,6 +244,7 @@
 
     hop1(0)
     hop1(1)
+    hop1(2)
 
     place, group = iota((GROUPS, 128), 1), iota((GROUPS, 128), 0)
     inv_vec[...] = jnp.zeros((8, 128), jnp.int32)
@@ -353,6 +354,7 @@
 
     route(0)
     route(1)
+    route(2)
 
     def swap_arrived(c):
         drain(q2.at[pl.ds(*CUTS[c])], zrecv.at[c])
@@ -401,7 +403,6 @@
     pending["across_1"] = on_right.wait_recv
     pending["across_2"] = on_left.wait_recv
     swap(0)
-    hop1(2)
     swap(1)
     finish("own_keys")
 
@@ -472,8 +473,6 @@
             copy.start()
             pending["back_sent", c, s] = copy.wait_send
             pending["back", c, s] = copy.wait_recv
-        if c == 0:
-            route(2)
     finish(("hop2", 2))
     extra = lines(q1, 4, 1, EP)
     for c in range(2):
@@ -488,6 +487,7 @@
         own_den.append(den)
         acc_own[HALF * c : HALF * (c + 1)] = acc
     finish("weights")
+    head_of = iota((HALF, 128), 0) % 8
     for c in range(2):
         finish(("back", c, 0), ("back", c, 1))
         at = slice(HALF * c, HALF * (c + 1))
@@ -499,11 +499,12 @@
         latent[at] = (
             acc_own[at] * (mine * scaled) + numer_in[c].astype(F32) * (theirs * scaled)
         ).astype(BF16)
-
-    head_of = iota((nq, 128), 0) % 8
-    for h in range(8):
-        value = jnp.dot(latent[...], wuv[h], preferred_element_type=F32)
-        flatm[:, h * 128 : (h + 1) * 128] = jnp.where(head_of == h, value, 0.0).astype(BF16)
+        for h in range(8):
+            value = jnp.dot(latent[at], wuv[h], preferred_element_type=F32)
+            flatm[at, h * 128 : (h + 1) * 128] = jnp.where(head_of == h, value, 0.0).astype(
+                BF16
+            )
+
     o, n = iota((ROWS, nq), 0), iota((ROWS, nq), 1)
     chosen = (n % HALF) // 16 == o % 12
     chosen = chosen & ((n // HALF) * 2 + (n // 8) % 2 == o // 12)
@@ -525,19 +526,33 @@
         pending["spread_sent", s] = lambda: drain(rs1.at[pl.ds(0, 7)], tsend.at[s])
         pending["spread", s] = lambda: drain(dst.at[pl.ds(0, 7)], trecv.at[s])
 
-    def slabs(left_side, weight, dst):
-        for j in range(4):
+    def slabs(left_side, weight, part, dst, s):
+        for dx in (2, 1, 3, 0):
+            pair = lax.rem(x + dx, 4)
+            columns = pl.ds(pl.multiple_of(pair * 2 * SLAB, 128), 2 * SLAB)
             wide = jnp.dot(
-                left_side, weight[:, 896 * j : 896 * (j + 1)], preferred_element_type=F32
+                left_side, weight[:, columns], preferred_element_type=F32
             ).astype(BF16)
-            dst[2 * j, :, :SLAB] = wide[:, :SLAB]
-            dst[2 * j + 1, :, :SLAB] = wide[:, SLAB:]
+            part[2 * pair, :, :SLAB] = wide[:, :SLAB]
+            part[2 * pair + 1, :, :SLAB] = wide[:, SLAB:]
+            for to in (pair * 2 + z, peer_t) if dx == 0 else (pair * 2, pair * 2 + 1):
+                if dx == 0 and to is not peer_t:
+                    dst[t] = part[t]
+                    continue
+                pltpu.make_async_remote_copy(
+                    src_ref=part.at[to],
+                    dst_ref=dst.at[t],
+                    send_sem=tsend.at[s],
+                    recv_sem=trecv.at[s],
+                    device_id={"tp": to},
+                    device_id_type=MESH,
+                ).start()
+        pending["spread_sent", s] = lambda: drain(rs1.at[pl.ds(0, 7)], tsend.at[s])
+        pending["spread", s] = lambda: drain(dst.at[pl.ds(0, 7)], trecv.at[s])
 
     mix[0, :, :, SLAB:] = jnp.zeros((8, ROWS, SLABW - SLAB), BF16)
     mix[1, :, :, SLAB:] = jnp.zeros((8, ROWS, SLABW - SLAB), BF16)
-    slabs(flat, wout, mix.at[0])
-    spread(lambda to: mix.at[0, to], rs1, 0)
-    rs1[t] = mix[0, t]
+    slabs(flat, wout, mix.at[0], rs1, 0)
     o, m = iota((ROWS, nt), 0), iota((ROWS, nt), 1)
     line = (m // 32) * 8 + m % 8
     chosen = (line - 12 == o % 12) & ((m // 8) % 4 == o // 12)
@@ -689,9 +704,7 @@
         blocks,
         preferred_element_type=F32,
     ).astype(BF16)
-    slabs(active, wdown, mix.at[1])
-    spread(lambda to: mix.at[1, to], rs2, 2)
-    rs2[t] = mix[1, t]
+    slabs(active, wdown, mix.at[1], rs2, 2)
     finish("home")
     finish(("spread", 2))
     summed = rs2[0].astype(F32)

time: 101 us -> 94.5 us (0.936)
  Pallas kernels: 99.2 us -> 92.9 us
    pallas_call x1, Pallas kernels: 99.2 us -> 92.9 us  [on_device(): pl.pallas_call(kernel, out_shape=jax.ShapeDtypeStruct((12, 4, SLAB), BF16...]
where the time goes in v8:
time: 94.5 us; the launch traced here: 94.3 us
  Pallas kernels  92.9 us (98%)
  local copies, waits for them, and re-layouts  1.44 us (2%)
    pallas_call x1, Pallas kernels, on_device(): pl.pallas_call(kernel, out_shape=jax.ShapeDtypeStruct((12, 4, SLAB), BF16...  92.9 us

profile of v8, /device:TPU:1, one launch (start us, length us, event | category | flops | bytes accessed | tf_op | source)
XLA Modules:
  0.0 94.3 jit_solution(10713275669688248133)
XLA Ops:
  0.0 92.9 %shard_map.127 = bf16[12,4,448]{2,1,0:T(4,128)(2,1)} custom-call(s32[4,32]{1,0:T(4,128)} %bitcast.5, s32[32,48]{1,0:T(8,128)} %table_ref.1, s32[12]{0:T(128)} %context_ref.1, s32[4,32]{1,0:T(4,128)} %bitcast.6, bf16[12,4,8,576]{3,2,1,0:T(8,128)(2,1)} %queries_ref.1, bf16[12,4,576]{2,1,0:T(4,128)(2,1)} %tail_ref.1, bf16[12,4,3584]{2,1,0:T(4,128)(2,1)} %resid_ref.1, ...), custom_call_target="tpu_custom_call" | custom-call | tf_op jit(solution)/shard_map/pallas_call | solution.py:747
  92.9 1.4 %copy.15 = bf16[12,4,448]{2,1,0:T(4,128)(2,1)} copy(bf16[12,4,448]{2,1,0:T(4,128)(2,1)} %shard_map.127) | data formatting | bytes 86016

commit v9 on v8

--- a/solution.py
+++ b/solution.py
@@ -211,58 +211,6 @@
 
     pl.semaphore_wait(barrier, GROUPS - 1 + 7 + 16)
 
-    def hop1_sent(c):
-        chunk = pl.ds(*CUTS[c])
-
-        @pl.when(g >= NP)
-        def _():
-            drain(send_ref.at[chunk, pl.ds(0, NP)], hsend.at[c])
-
-        @pl.when(g < NP)
-        def _():
-            drain(send_ref.at[chunk, pl.ds(0, NP - 1)], hsend.at[c])
-
-    def hop1(c):
-        chunk = pl.ds(*CUTS[c])
-
-        @pl.loop(1, GROUPS)
-        def _(d):
-            to = lax.rem(g + d, GROUPS)
-
-            @pl.when(to < NP)
-            def _():
-                pltpu.make_async_remote_copy(
-                    src_ref=send_ref.at[chunk, to],
-                    dst_ref=h1[c].at[:, g],
-                    send_sem=hsend.at[c],
-                    recv_sem=hrecv.at[c],
-                    device_id={"grp": to},
-                    device_id_type=MESH,
-                ).start()
-
-        pending["hop1_sent", c] = functools.partial(hop1_sent, c)
-
-    hop1(0)
-    hop1(1)
-    hop1(2)
-
-    place, group = iota((GROUPS, 128), 1), iota((GROUPS, 128), 0)
-    inv_vec[...] = jnp.zeros((8, 128), jnp.int32)
-    columns = reads_vec[...].T
-    for k in range(4):
-        asked_here = columns[:, k : k + 1] == place
-        inv_vec[k : k + 1, :] = jnp.max(
-            jnp.where(asked_here, group, 0), axis=0, keepdims=True
-        )
-    askers = pltpu.make_async_copy(inv_vec, inv_ref, wsem.at[6])
-    askers.start()
-    offset = iota((1, 128), 1)
-    for j in range(48):
-        pos_ref[j // 6, :, (j % 6) * 128 : (j % 6 + 1) * 128] = (
-            table_ref[g, j] * 128 + offset
-        ).astype(F32)
-    askers.wait()
-
     to_right = pltpu.make_async_remote_copy(
         src_ref=pool_ref,
         dst_ref=kbuf.at[x],
@@ -285,6 +233,58 @@
     pending["left_sent"] = to_left.wait_send
     pending["from_left"] = to_right.wait_recv
     pending["from_right"] = to_left.wait_recv
+
+    def hop1_sent(c):
+        chunk = pl.ds(*CUTS[c])
+
+        @pl.when(g >= NP)
+        def _():
+            drain(send_ref.at[chunk, pl.ds(0, NP)], hsend.at[c])
+
+        @pl.when(g < NP)
+        def _():
+            drain(send_ref.at[chunk, pl.ds(0, NP - 1)], hsend.at[c])
+
+    def hop1(c):
+        chunk = pl.ds(*CUTS[c])
+
+        @pl.loop(1, GROUPS)
+        def _(d):
+            to = lax.rem(g + d, GROUPS)
+
+            @pl.when(to < NP)
+            def _():
+                pltpu.make_async_remote_copy(
+                    src_ref=send_ref.at[chunk, to],
+                    dst_ref=h1[c].at[:, g],
+                    send_sem=hsend.at[c],
+                    recv_sem=hrecv.at[c],
+                    device_id={"grp": to},
+                    device_id_type=MESH,
+                ).start()
+
+        pending["hop1_sent", c] = functools.partial(hop1_sent, c)
+
+    hop1(0)
+    hop1(1)
+    hop1(2)
+
+    place, group = iota((GROUPS, 128), 1), iota((GROUPS, 128), 0)
+    inv_vec[...] = jnp.zeros((8, 128), jnp.int32)
+    columns = reads_vec[...].T
+    for k in range(4):
+        asked_here = columns[:, k : k + 1] == place
+        inv_vec[k : k + 1, :] = jnp.max(
+            jnp.where(asked_here, group, 0), axis=0, keepdims=True
+        )
+    askers = pltpu.make_async_copy(inv_vec, inv_ref, wsem.at[6])
+    askers.start()
+    offset = iota((1, 128), 1)
+    for j in range(48):
+        pos_ref[j // 6, :, (j % 6) * 128 : (j % 6 + 1) * 128] = (
+            table_ref[g, j] * 128 + offset
+        ).astype(F32)
+    askers.wait()
 
     def hop2_sent(c):
         @pl.when(g < NP)
@@ -513,8 +513,8 @@
     ).astype(BF16)
 
     def spread(part, dst, s):
-        for d in range(1, 8):
-            to = lax.rem(t + d, 8)
+        for dx, dz in ((2, 1), (1, 1), (3, 1), (2, 0), (0, 1), (1, 0), (3, 0)):
+            to = lax.rem(x + dx, 4) * 2 + lax.rem(z + dz, 2)
             pltpu.make_async_remote_copy(
                 src_ref=part(to),
                 dst_ref=dst.at[t],

time: 94.5 us -> 94.3 us (level)
  no operation moved by 1% of the time
where the time goes in v9:
time: 94.3 us; the launch traced here: 94.2 us
  Pallas kernels  92.7 us (98%)
  local copies, waits for them, and re-layouts  1.44 us (2%)
    pallas_call x1, Pallas kernels, on_device(): pl.pallas_call(kernel, out_shape=jax.ShapeDtypeStruct((12, 4, SLAB), BF16...  92.7 us

profile of v9, /device:TPU:1, one launch (start us, length us, event | category | flops | bytes accessed | tf_op | source)
XLA Modules:
  0.0 94.2 jit_solution(13872196379952659807)
XLA Ops:
  0.0 92.7 %shard_map.127 = bf16[12,4,448]{2,1,0:T(4,128)(2,1)} custom-call(s32[4,32]{1,0:T(4,128)} %bitcast.5, s32[32,48]{1,0:T(8,128)} %table_ref.1, s32[12]{0:T(128)} %context_ref.1, s32[4,32]{1,0:T(4,128)} %bitcast.6, bf16[12,4,8,576]{3,2,1,0:T(8,128)(2,1)} %queries_ref.1, bf16[12,4,576]{2,1,0:T(4,128)(2,1)} %tail_ref.1, bf16[12,4,3584]{2,1,0:T(4,128)(2,1)} %resid_ref.1, ...), custom_call_target="tpu_custom_call" | custom-call | tf_op jit(solution)/shard_map/pallas_call | solution.py:747
  92.7 1.4 %copy.15 = bf16[12,4,448]{2,1,0:T(4,128)(2,1)} copy(bf16[12,4,448]{2,1,0:T(4,128)(2,1)} %shard_map.127) | data formatting | bytes 86016
